TPU v7x, 512 devices: a whole 4x4x16 slice. The times are simulated.
512 devices in a mesh: ctx: 64 (over z, x), kvh: 8 (over y, core).
Axes of the slice: x: 4, y: 4, z: 16, core: 2. Of those that a mesh axis runs over, the one named last changes fastest.
Arguments:
- doc_lengths: int32 [64], replicated, may hold values from 1 to 384, 16384 in all
- queries: bfloat16 [2, 8192, 8192], P(None, ('ctx', 'kvh')), may hold values from -6 to 6
- key_matrix: bfloat16 [2, 8192, 1024], P(None, ('ctx', 'kvh')), may hold values from -6 to 6
- value_matrix: bfloat16 [2, 8192, 1024], P(None, ('ctx', 'kvh')), may hold values from -6 to 6
- forward_output: bfloat16 [2, 8192, 8192], P(None, ('ctx', 'kvh')), may hold values from -6 to 6
- output_cotangent: bfloat16 [2, 8192, 8192], P(None, ('ctx', 'kvh')), may hold values from -0.59765625 to 0.59765625
- log_normalizer_rows: float32 [2, 8192, 64], P(None, ('ctx', 'kvh')), may hold values from 1.5 to 3
Outputs:
- query_gradient: bfloat16 [2, 8192, 8192], P(None, 'ctx', 'kvh')
- key_gradient: bfloat16 [2, 8192, 1024], P(None, 'ctx', 'kvh')
- value_gradient: bfloat16 [2, 8192, 1024], P(None, 'ctx', 'kvh')
Inputs may be any that keep to these rules, and one draw needn't show every extreme that they name: `doc_lengths`: the documents fill the pack of 16384 positions end to end; the longest has exactly 384 tokens.
All inputs are finite; a program needn't handle non-finite values.
Results may differ from a plain program's by a relative error of at most 0.0054.
Values may be sent and summed in bfloat16 or wider, within the bound.
No kernel may reach another device: no remote copies, remote signals or barrier semaphores. Data moves between devices by JAX's collectives and lax.ppermute only.
A program may use at most 64 MiB of HBM per device.

v0:
```python
from functools import partial

import jax
import jax.numpy as jnp
from jax import lax
from jax.sharding import PartitionSpec as P

QUERY_PER_GROUP = 8
HEAD_SIZE = 128
LOOK = 3


def padded(block, sides, width):
    for axis, dim in sides:
        count = lax.axis_size(axis)
        forward = [(i, i + 1) for i in range(count - 1)]
        backward = [(target, source) for source, target in forward]
        low = lax.ppermute(
            lax.slice_in_dim(block, block.shape[dim] - width, None, axis=dim), axis, forward
        )
        high = lax.ppermute(lax.slice_in_dim(block, 0, width, axis=dim), axis, backward)
        block = jnp.concatenate([low, block, high], axis=dim)
    return block


def block_docs(doc_ends, block_ids, block_len):
    position = block_ids[:, None] * block_len + jnp.arange(block_len, dtype=jnp.int32)[None, :]
    doc_ids = jnp.sum((doc_ends[None, None, :] <= position[:, :, None]).astype(jnp.int32), axis=2)
    return (jnp.where(block_ids[:, None] >= 0, doc_ids, -1), position)


def tile_grads(query_rows, grad_rows, norm_rows, delta_rows, tile_pair, allowed):
    inv_root = HEAD_SIZE ** (-0.5)
    key_tile = tile_pair[..., :HEAD_SIZE]
    value_tile = tile_pair[..., HEAD_SIZE:]
    scores = (
        jnp.einsum("hqgd,hkd->hgqk", query_rows, key_tile, preferred_element_type=jnp.float32)
        * inv_root
    )
    weights = jnp.where(allowed[:, None], jnp.exp(scores - norm_rows[..., None]), 0.0)
    weight_bf = weights.astype(jnp.bfloat16)
    value_gradient = jnp.einsum(
        "hgqk,hqgd->hkd", weight_bf, grad_rows, preferred_element_type=jnp.float32
    )
    weight_grad = jnp.einsum(
        "hqgd,hkd->hgqk", grad_rows, value_tile, preferred_element_type=jnp.float32
    )
    score_bf = (weights * (weight_grad - delta_rows[..., None])).astype(jnp.bfloat16)
    query_gradient = (
        jnp.einsum("hgqk,hkd->hqgd", score_bf, key_tile, preferred_element_type=jnp.float32)
        * inv_root
    )
    key_gradient = (
        jnp.einsum("hgqk,hqgd->hkd", score_bf, query_rows, preferred_element_type=jnp.float32)
        * inv_root
    )
    return (query_gradient, jnp.concatenate([key_gradient, value_gradient], axis=-1))


def body(
    doc_lengths,
    queries,
    key_matrix,
    value_matrix,
    forward_output,
    output_cotangent,
    log_normalizer_rows,
):
    head_shape = forward_output.shape[:2] + (forward_output.shape[2] // HEAD_SIZE, HEAD_SIZE)
    delta_local = jnp.sum(
        forward_output.reshape(head_shape).astype(jnp.float32)
        * output_cotangent.reshape(head_shape).astype(jnp.float32),
        axis=-1,
    )
    query_heads, key_heads, value_heads, grad_heads = (
        lax.all_to_all(queries, "kvh", split_axis=2, concat_axis=1, tiled=True),
        lax.all_to_all(key_matrix, "kvh", split_axis=2, concat_axis=1, tiled=True),
        lax.all_to_all(value_matrix, "kvh", split_axis=2, concat_axis=1, tiled=True),
        lax.all_to_all(output_cotangent, "kvh", split_axis=2, concat_axis=1, tiled=True),
    )
    norm_heads, delta_heads = (
        lax.all_to_all(log_normalizer_rows, "kvh", split_axis=2, concat_axis=1, tiled=True),
        lax.all_to_all(delta_local, "kvh", split_axis=2, concat_axis=1, tiled=True),
    )
    block_len = key_heads.shape[1]
    ctx_count = lax.axis_size("ctx")
    ctx_index = lax.axis_index("ctx")
    at_fold = ctx_index == ctx_count - 1
    query_rows = query_heads.reshape(2, block_len, QUERY_PER_GROUP, HEAD_SIZE)
    grad_rows = grad_heads.reshape(2, block_len, QUERY_PER_GROUP, HEAD_SIZE)
    norm_rows = jnp.transpose(norm_heads, (0, 2, 1))
    delta_rows = jnp.transpose(delta_heads, (0, 2, 1))
    doc_ends = jnp.cumsum(doc_lengths)
    own_blocks = jnp.stack([ctx_index, 2 * ctx_count - 1 - ctx_index])
    query_docs, query_pos = block_docs(doc_ends, own_blocks, block_len)
    key_pair = jnp.concatenate([key_heads, value_heads], axis=-1)
    key_tiles = [key_pair]
    for lookback in range(LOOK):
        rimmed = padded(jnp.stack([key_pair[1], key_pair[0]]), (("ctx", 0),), 1)
        key_pair = jnp.stack([rimmed[0], jnp.where(at_fold, key_pair[0], rimmed[3])])
        key_tiles.append(key_pair)
    query_total = jnp.zeros((2, block_len, QUERY_PER_GROUP, HEAD_SIZE), jnp.float32)
    partials = []
    for lookback in range(LOOK + 1):
        tile_pair = key_tiles[lookback]
        tile_docs, tile_pos = block_docs(doc_ends, own_blocks - lookback, block_len)
        same_doc = query_docs[:, :, None] == tile_docs[:, None, :]
        allowed = same_doc & (tile_pos[:, None, :] <= query_pos[:, :, None])
        compute = partial(
            tile_grads, query_rows, grad_rows, norm_rows, delta_rows, tile_pair, allowed
        )
        query_part, pair_grad = compute()
        query_total = query_total + query_part
        partials.append(pair_grad)
    returned = partials[LOOK]
    for lookback in range(LOOK - 1, -1, -1):
        rimmed = padded(returned, (("ctx", 0),), 1)
        lower_rows = jnp.where(at_fold, returned[1], rimmed[3])
        returned = jnp.stack([lower_rows, rimmed[0]]) + partials[lookback]
    query_gradient = query_total.reshape(2, block_len, QUERY_PER_GROUP * HEAD_SIZE).astype(
        jnp.bfloat16
    )
    return (
        query_gradient,
        returned[..., :HEAD_SIZE].astype(jnp.bfloat16),
        returned[..., HEAD_SIZE:].astype(jnp.bfloat16),
    )


def solution(mesh):
    placed = (
        P(),
        P(None, ("ctx", "kvh"), None),
        P(None, ("ctx", "kvh"), None),
        P(None, ("ctx", "kvh"), None),
        P(None, ("ctx", "kvh"), None),
        P(None, ("ctx", "kvh"), None),
        P(None, ("ctx", "kvh"), None),
    )
    return jax.shard_map(
        body,
        mesh=mesh,
        in_specs=placed,
        out_specs=(P(None, "ctx", "kvh"), P(None, "ctx", "kvh"), P(None, "ctx", "kvh")),
        check_vma=False,
    )
```

profile of v0, /device:TPU:384, one launch (start us, length us, event | category | flops | bytes accessed | tf_op | source)
XLA Modules:
  0.0 189.3 jit_solution(7647184871618518229)
XLA Ops:
  0.7 1.2 copy.208
  1.8 1.2 reshape.446
  3.0 4.5 %all-to-all-start.3 = ((bf16[8,2,2048]{2,1,0:T(2,128)(2,1)}), bf16[8,2,2048]{2,1,0:T(2,128)(2,1)S(1)}, u32[]{:S(2)}, u32[]{:S(2)}) async-start(bf16[8,2,2048]{2,1,0:T(2,128)(2,1)} %reshape.446), calls=%async_computation.3 | async-start | bytes 131072 | tf_op jit(solution)/shard_map/all_to_all | solution.py:78
  7.6 0.7 copy.199
  8.7 1.3 convert_multiply_fusion
  10.2 1.1 copy.200
  11.3 1.2 reshape.440
  13.1 4.2 %all-to-all-start = ((bf16[8,2,2048]{2,1,0:T(2,128)(2,1)}), bf16[8,2,2048]{2,1,0:T(2,128)(2,1)S(1)}, u32[]{:S(2)}, u32[]{:S(2)}) async-start(bf16[8,2,2048]{2,1,0:T(2,128)(2,1)} %reshape.440), calls=%async_computation | async-start | bytes 131072 | tf_op jit(solution)/shard_map/all_to_all | solution.py:77
  17.5 0.7 reshape.444
  18.4 4.5 %all-to-all-done = bf16[8,2,2048]{2,1,0:T(2,128)(2,1)S(1)} async-done(((bf16[8,2,2048]{2,1,0:T(2,128)(2,1)}), bf16[8,2,2048]{2,1,0:T(2,128)(2,1)S(1)}, u32[]{:S(2)}, u32[]{:S(2)}) %all-to-all-start) | async-done | bytes 65568 | tf_op jit(solution)/shard_map/all_to_all | solution.py:77
  22.9 3.3 %all-to-all-start.2 = ((f32[8,1,256]{2,1,0:T(1,128)}), f32[8,1,256]{2,1,0:T(1,128)S(1)}, u32[]{:S(2)}, u32[]{:S(2)}) async-start(f32[8,1,256]{2,1,0:T(1,128)} %reshape.444), calls=%async_computation.2 | async-start | bytes 16384 | tf_op jit(solution)/shard_map/all_to_all | solution.py:82
  26.6 6.7 %copy.202 = bf16[2,16,8192]{1,0,2:T(2,128)(2,1)} copy(bf16[2,16,8192]{2,1,0:T(8,128)(2,1)S(1)} %copy-done.15) | data formatting | bytes 1048576 | tf_op args[1]
  33.3 6.5 %reshape.442 = bf16[8,2,16384]{2,1,0:T(2,128)(2,1)} reshape(bf16[8192,2,16]{2,1,0:T(2,128)(2,1)} %bitcast.250) | data formatting | bytes 1048576
  39.9 0.7 reshape.450
  42.1 4.7 %all-to-all-start.5 = ((f32[8,1,256]{2,1,0:T(1,128)}), f32[8,1,256]{2,1,0:T(1,128)S(1)}, u32[]{:S(2)}, u32[]{:S(2)}) async-start(f32[8,1,256]{2,1,0:T(1,128)} %reshape.450), calls=%async_computation.5 | async-start | bytes 16384 | tf_op jit(solution)/shard_map/all_to_all | solution.py:83
  46.9 6.3 %collective-permute-start.1 = (bf16[1,128,256]{2,1,0:T(8,128)(2,1)S(1)}, bf16[1,128,256]{2,1,0:T(8,128)(2,1)S(1)}, u32[]{:S(2)}, u32[]{:S(2)}) collective-permute-start(bf16[1,128,256]{2,1,0:T(8,128)(2,1)S(1)} %pad_maximum_fusion.4), channel_id=1, source_target_pairs={{8,0},{16,8},{24,16},{32,24},{40,32},{48,40},{56,48},{64,56},{72,6... | collective-permute-start | bytes 196616 | tf_op jit(solution)/shard_map/ppermute | solution.py:21
  53.2 4.8 %all-to-all-start.1 = ((bf16[8,2,16384]{2,1,0:T(2,128)(2,1)}), bf16[8,2,16384]{2,1,0:T(2,128)(2,1)S(1)}, u32[]{:S(2)}, u32[]{:S(2)}) async-start(bf16[8,2,16384]{2,1,0:T(2,128)(2,1)} %reshape.442), calls=%async_computation.1 | async-start | bytes 1048576 | tf_op jit(solution)/shard_map/all_to_all | solution.py:76
  58.1 1.9 %collective-permute-start = (bf16[1,128,256]{2,1,0:T(8,128)(2,1)S(1)}, bf16[1,128,256]{2,1,0:T(8,128)(2,1)S(1)}, u32[]{:S(2)}, u32[]{:S(2)}) collective-permute-start(bf16[1,128,256]{2,1,0:T(8,128)(2,1)S(1)} %get-tuple-element.27), channel_id=1, source_target_pairs={{0,8},{8,16},{16,24},{24,32},{32,40},{40,48},{48,56},{56,64},{64,7... | collective-permute-start | bytes 196616 | tf_op jit(solution)/shard_map/ppermute | solution.py:18
  60.1 7.2 %collective-permute-start.3 = (bf16[1,128,256]{2,1,0:T(8,128)(2,1)S(1)}, bf16[1,128,256]{2,1,0:T(8,128)(2,1)S(1)}, u32[]{:S(2)}, u32[]{:S(2)}) collective-permute-start(bf16[1,128,256]{2,1,0:T(8,128)(2,1)S(1)} %get-tuple-element.26), channel_id=1, source_target_pairs={{8,0},{16,8},{24,16},{32,24},{40,32},{48,40},{56,48},{64,56},{72,6... | collective-permute-start | bytes 196616 | tf_op jit(solution)/shard_map/ppermute | solution.py:21
  67.4 6.7 %copy.210 = bf16[2,16,8192]{1,0,2:T(2,128)(2,1)} copy(bf16[2,16,8192]{2,1,0:T(8,128)(2,1)S(1)} %copy-done.6) | data formatting | bytes 1048576 | tf_op args[5]
  74.1 6.5 %reshape.448 = bf16[8,2,16384]{2,1,0:T(2,128)(2,1)} reshape(bf16[8192,2,16]{2,1,0:T(2,128)(2,1)} %bitcast.251) | data formatting | bytes 1048576
  80.6 4.8 %all-to-all-start.4 = ((bf16[8,2,16384]{2,1,0:T(2,128)(2,1)}), bf16[8,2,16384]{2,1,0:T(2,128)(2,1)S(1)}, u32[]{:S(2)}, u32[]{:S(2)}) async-start(bf16[8,2,16384]{2,1,0:T(2,128)(2,1)} %reshape.448), calls=%async_computation.4 | async-start | bytes 1048576 | tf_op jit(solution)/shard_map/all_to_all | solution.py:79
  85.4 1.9 %collective-permute-start.5 = (bf16[1,128,256]{2,1,0:T(8,128)(2,1)S(1)}, bf16[1,128,256]{2,1,0:T(8,128)(2,1)S(1)}, u32[]{:S(2)}, u32[]{:S(2)}) collective-permute-start(bf16[1,128,256]{2,1,0:T(8,128)(2,1)S(1)} %broadcast_select_fusion.4), channel_id=1, source_target_pairs={{8,0},{16,8},{24,16},{32,24},{40,32},{48,40},{56,48},{64,56},{72,6... | collective-permute-start | bytes 196616 | tf_op jit(solution)/shard_map/ppermute | solution.py:21
  87.3 3.9 %collective-permute-start.2 = (bf16[1,128,256]{2,1,0:T(8,128)(2,1)S(1)}, bf16[1,128,256]{2,1,0:T(8,128)(2,1)S(1)}, u32[]{:S(2)}, u32[]{:S(2)}) collective-permute-start(bf16[1,128,256]{2,1,0:T(8,128)(2,1)S(1)} %collective-permute-done), channel_id=1, source_target_pairs={{0,8},{8,16},{16,24},{24,32},{32,40},{40,48},{48,56},{56,64},{64,7... | collective-permute-start | bytes 196616 | tf_op jit(solution)/shard_map/ppermute | solution.py:18
  91.3 1.0 compare_and_fusion
  94.6 2.4 %collective-permute-done.2 = bf16[1,128,256]{2,1,0:T(8,128)(2,1)S(1)} collective-permute-done((bf16[1,128,256]{2,1,0:T(8,128)(2,1)S(1)}, bf16[1,128,256]{2,1,0:T(8,128)(2,1)S(1)}, u32[]{:S(2)}, u32[]{:S(2)}) %collective-permute-start.2) | collective-permute-done | bytes 65568 | tf_op jit(solution)/shard_map/ppermute | solution.py:18
  97.0 1.9 %collective-permute-start.4 = (bf16[1,128,256]{2,1,0:T(8,128)(2,1)S(1)}, bf16[1,128,256]{2,1,0:T(8,128)(2,1)S(1)}, u32[]{:S(2)}, u32[]{:S(2)}) collective-permute-start(bf16[1,128,256]{2,1,0:T(8,128)(2,1)S(1)} %collective-permute-done.2), channel_id=1, source_target_pairs={{0,8},{8,16},{16,24},{24,32},{32,40},{40,48},{48,56},{56,64},{64,7... | collective-permute-start | bytes 196616 | tf_op jit(solution)/shard_map/ppermute | solution.py:18
  99.0 4.1 %reshape.443 = bf16[8192,2,16]{2,1,0:T(2,128)(2,1)} reshape(bf16[8,2,16384]{2,1,0:T(2,128)(2,1)S(1)} %all-to-all-done.1) | data formatting | bytes 1048576
  103.1 8.9 %copy.203 = bf16[2,16,8,1024]{3,1,2,0:T(8,128)(2,1)S(1)} copy(bf16[2,16,8,1024]{1,0,3,2:T(2,128)(2,1)} %bitcast.248) | data formatting | bytes 1048576 | tf_op jit(solution)/shard_map/all_to_all | solution.py:76
  112.5 4.1 %reshape.449 = bf16[8192,2,16]{2,1,0:T(2,128)(2,1)} reshape(bf16[8,2,16384]{2,1,0:T(2,128)(2,1)S(1)} %all-to-all-done.4) | data formatting | bytes 1048576
  116.6 8.9 %copy.211 = bf16[2,16,8,1024]{3,1,2,0:T(8,128)(2,1)S(1)} copy(bf16[2,16,8,1024]{1,0,3,2:T(2,128)(2,1)} %bitcast.249) | data formatting | bytes 1048576 | tf_op jit(solution)/shard_map/all_to_all | solution.py:79
  128.0 7.4 %collective-permute-start.6 = (f32[1,128,256]{2,1,0:T(8,128)}, f32[1,128,256]{2,1,0:T(8,128)}, u32[]{:S(2)}, u32[]{:S(2)}) collective-permute-start(f32[1,128,256]{2,1,0:T(8,128)} %pad_maximum_fusion), channel_id=1, source_target_pairs={{8,0},{16,8},{24,16},{32,24},{40,32},{48,40},{56,48},{64,56},{72,6... | collective-permute-start | bytes 393224 | tf_op jit(solution)/shard_map/ppermute | solution.py:21
  138.6 1.2 fusion.31
  139.7 2.0 %copy.254 = bf16[2,128,1024]{2,1,0:T(8,128)(2,1)} copy(bf16[2,128,1024]{1,2,0:T(8,128)(2,1)} %bitcast.254) | data formatting | bytes 1048576
  141.8 1.4 fusion.37
  143.2 1.0 broadcast_select_fusion.2
  144.2 1.9 %collective-permute-start.7 = (f32[1,128,256]{2,1,0:T(8,128)S(1)}, f32[1,128,256]{2,1,0:T(8,128)S(1)}, u32[]{:S(2)}, u32[]{:S(2)}) collective-permute-start(f32[1,128,256]{2,1,0:T(8,128)S(1)} %get-tuple-element.23), channel_id=1, source_target_pairs={{0,8},{8,16},{16,24},{24,32},{32,40},{40,48},{48,56},{56,64},{64,7... | collective-permute-start | bytes 393224 | tf_op jit(solution)/shard_map/ppermute | solution.py:18
  146.1 1.5 convolution_bitcast_fusion.8
  147.6 6.7 %collective-permute-done.7 = f32[1,128,256]{2,1,0:T(8,128)S(1)} collective-permute-done((f32[1,128,256]{2,1,0:T(8,128)S(1)}, f32[1,128,256]{2,1,0:T(8,128)S(1)}, u32[]{:S(2)}, u32[]{:S(2)}) %collective-permute-start.7) | collective-permute-done | bytes 131104 | tf_op jit(solution)/shard_map/ppermute | solution.py:18
  154.4 1.9 %collective-permute-start.8 = (f32[1,128,256]{2,1,0:T(8,128)S(1)}, f32[1,128,256]{2,1,0:T(8,128)S(1)}, u32[]{:S(2)}, u32[]{:S(2)}) collective-permute-start(f32[1,128,256]{2,1,0:T(8,128)S(1)} %slice.81), channel_id=1, source_target_pairs={{8,0},{16,8},{24,16},{32,24},{40,32},{48,40},{56,48},{64,56},{72,6... | collective-permute-start | bytes 393224 | tf_op jit(solution)/shard_map/ppermute | solution.py:21
  156.7 4.6 %collective-permute-done.8 = f32[1,128,256]{2,1,0:T(8,128)S(1)} collective-permute-done((f32[1,128,256]{2,1,0:T(8,128)S(1)}, f32[1,128,256]{2,1,0:T(8,128)S(1)}, u32[]{:S(2)}, u32[]{:S(2)}) %collective-permute-start.8) | collective-permute-done | bytes 131104 | tf_op jit(solution)/shard_map/ppermute | solution.py:21
  161.3 1.9 %collective-permute-start.9 = (f32[1,128,256]{2,1,0:T(8,128)S(1)}, f32[1,128,256]{2,1,0:T(8,128)S(1)}, u32[]{:S(2)}, u32[]{:S(2)}) collective-permute-start(f32[1,128,256]{2,1,0:T(8,128)S(1)} %get-tuple-element.31), channel_id=1, source_target_pairs={{0,8},{8,16},{16,24},{24,32},{32,40},{40,48},{48,56},{56,64},{64,7... | collective-permute-start | bytes 393224 | tf_op jit(solution)/shard_map/ppermute | solution.py:18
  163.5 8.0 %collective-permute-done.9 = f32[1,128,256]{2,1,0:T(8,128)S(1)} collective-permute-done((f32[1,128,256]{2,1,0:T(8,128)S(1)}, f32[1,128,256]{2,1,0:T(8,128)S(1)}, u32[]{:S(2)}, u32[]{:S(2)}) %collective-permute-start.9) | collective-permute-done | bytes 131104 | tf_op jit(solution)/shard_map/ppermute | solution.py:18
  171.5 1.9 %collective-permute-start.10 = (f32[1,128,256]{2,1,0:T(8,128)S(1)}, f32[1,128,256]{2,1,0:T(8,128)S(1)}, u32[]{:S(2)}, u32[]{:S(2)}) collective-permute-start(f32[1,128,256]{2,1,0:T(8,128)S(1)} %slice.83), channel_id=1, source_target_pairs={{8,0},{16,8},{24,16},{32,24},{40,32},{48,40},{56,48},{64,56},{72,6... | collective-permute-start | bytes 393224 | tf_op jit(solution)/shard_map/ppermute | solution.py:21
  173.8 4.6 %collective-permute-done.10 = f32[1,128,256]{2,1,0:T(8,128)S(1)} collective-permute-done((f32[1,128,256]{2,1,0:T(8,128)S(1)}, f32[1,128,256]{2,1,0:T(8,128)S(1)}, u32[]{:S(2)}, u32[]{:S(2)}) %collective-permute-start.10) | collective-permute-done | bytes 131104 | tf_op jit(solution)/shard_map/ppermute | solution.py:21
  178.4 1.9 %collective-permute-start.11 = (f32[1,128,256]{2,1,0:T(8,128)S(1)}, f32[1,128,256]{2,1,0:T(8,128)S(1)}, u32[]{:S(2)}, u32[]{:S(2)}) collective-permute-start(f32[1,128,256]{2,1,0:T(8,128)S(1)} %get-tuple-element.29), channel_id=1, source_target_pairs={{0,8},{8,16},{16,24},{24,32},{32,40},{40,48},{48,56},{56,64},{64,7... | collective-permute-start | bytes 393224 | tf_op jit(solution)/shard_map/ppermute | solution.py:18
  180.6 8.0 %collective-permute-done.11 = f32[1,128,256]{2,1,0:T(8,128)S(1)} collective-permute-done((f32[1,128,256]{2,1,0:T(8,128)S(1)}, f32[1,128,256]{2,1,0:T(8,128)S(1)}, u32[]{:S(2)}, u32[]{:S(2)}) %collective-permute-start.11) | collective-permute-done | bytes 131104 | tf_op jit(solution)/shard_map/ppermute | solution.py:18
  188.6 0.7 fusion.79
  (113 shorter events, 13.1 us)
Async XLA Ops:
  0.6 16.7 %copy-start.18 = (f32[2,16,64]{2,1,0:T(8,128)S(1)}, f32[2,16,64]{2,1,0:T(8,128)}, u32[]{:S(2)}) copy-start(f32[2,16,64]{2,1,0:T(8,128)} %param.13) | copy-start | bytes 24580
  0.6 26.0 %copy-start.15 = (bf16[2,16,8192]{2,1,0:T(8,128)(2,1)S(1)}, bf16[2,16,8192]{2,1,0:T(8,128)(2,1)}, u32[]{:S(2)}) copy-start(bf16[2,16,8192]{2,1,0:T(8,128)(2,1)} %param.8) | copy-start | bytes 1572868
  3.0 10.1 %all-to-all-start.3 = ((bf16[8,2,2048]{2,1,0:T(2,128)(2,1)}), bf16[8,2,2048]{2,1,0:T(2,128)(2,1)S(1)}, u32[]{:S(2)}, u32[]{:S(2)}) async-start(bf16[8,2,2048]{2,1,0:T(2,128)(2,1)} %reshape.446), calls=%async_computation.3 | async-start | bytes 131072 | tf_op jit(solution)/shard_map/all_to_all | solution.py:78
  13.1 9.8 %all-to-all-start = ((bf16[8,2,2048]{2,1,0:T(2,128)(2,1)}), bf16[8,2,2048]{2,1,0:T(2,128)(2,1)S(1)}, u32[]{:S(2)}, u32[]{:S(2)}) async-start(bf16[8,2,2048]{2,1,0:T(2,128)(2,1)} %reshape.440), calls=%async_computation | async-start | bytes 131072 | tf_op jit(solution)/shard_map/all_to_all | solution.py:77
  22.9 19.2 %all-to-all-start.2 = ((f32[8,1,256]{2,1,0:T(1,128)}), f32[8,1,256]{2,1,0:T(1,128)S(1)}, u32[]{:S(2)}, u32[]{:S(2)}) async-start(f32[8,1,256]{2,1,0:T(1,128)} %reshape.444), calls=%async_computation.2 | async-start | bytes 16384 | tf_op jit(solution)/shard_map/all_to_all | solution.py:82
  33.3 34.1 %copy-start.6 = (bf16[2,16,8192]{2,1,0:T(8,128)(2,1)S(1)}, bf16[2,16,8192]{2,1,0:T(8,128)(2,1)}, u32[]{:S(2)}) copy-start(bf16[2,16,8192]{2,1,0:T(8,128)(2,1)} %param.12) | copy-start | bytes 1572868
  42.1 11.1 %all-to-all-start.5 = ((f32[8,1,256]{2,1,0:T(1,128)}), f32[8,1,256]{2,1,0:T(1,128)S(1)}, u32[]{:S(2)}, u32[]{:S(2)}) async-start(f32[8,1,256]{2,1,0:T(1,128)} %reshape.450), calls=%async_computation.5 | async-start | bytes 16384 | tf_op jit(solution)/shard_map/all_to_all | solution.py:83
  46.9 11.2 %collective-permute-start.1 = (bf16[1,128,256]{2,1,0:T(8,128)(2,1)S(1)}, bf16[1,128,256]{2,1,0:T(8,128)(2,1)S(1)}, u32[]{:S(2)}, u32[]{:S(2)}) collective-permute-start(bf16[1,128,256]{2,1,0:T(8,128)(2,1)S(1)} %pad_maximum_fusion.4), channel_id=1, source_target_pairs={{8,0},{16,8},{24,16},{32,24},{40,32},{48,40},{56,48},{64,56},{72,6... | collective-permute-start | bytes 196616 | tf_op jit(solution)/shard_map/ppermute | solution.py:21
  53.2 27.3 %all-to-all-start.1 = ((bf16[8,2,16384]{2,1,0:T(2,128)(2,1)}), bf16[8,2,16384]{2,1,0:T(2,128)(2,1)S(1)}, u32[]{:S(2)}, u32[]{:S(2)}) async-start(bf16[8,2,16384]{2,1,0:T(2,128)(2,1)} %reshape.442), calls=%async_computation.1 | async-start | bytes 1048576 | tf_op jit(solution)/shard_map/all_to_all | solution.py:76
  58.1 27.2 %collective-permute-start = (bf16[1,128,256]{2,1,0:T(8,128)(2,1)S(1)}, bf16[1,128,256]{2,1,0:T(8,128)(2,1)S(1)}, u32[]{:S(2)}, u32[]{:S(2)}) collective-permute-start(bf16[1,128,256]{2,1,0:T(8,128)(2,1)S(1)} %get-tuple-element.27), channel_id=1, source_target_pairs={{0,8},{8,16},{16,24},{24,32},{32,40},{40,48},{48,56},{56,64},{64,7... | collective-permute-start | bytes 196616 | tf_op jit(solution)/shard_map/ppermute | solution.py:18
  60.1 25.3 %collective-permute-start.3 = (bf16[1,128,256]{2,1,0:T(8,128)(2,1)S(1)}, bf16[1,128,256]{2,1,0:T(8,128)(2,1)S(1)}, u32[]{:S(2)}, u32[]{:S(2)}) collective-permute-start(bf16[1,128,256]{2,1,0:T(8,128)(2,1)S(1)} %get-tuple-element.26), channel_id=1, source_target_pairs={{8,0},{16,8},{24,16},{32,24},{40,32},{48,40},{56,48},{64,56},{72,6... | collective-permute-start | bytes 196616 | tf_op jit(solution)/shard_map/ppermute | solution.py:21
  80.6 32.0 %all-to-all-start.4 = ((bf16[8,2,16384]{2,1,0:T(2,128)(2,1)}), bf16[8,2,16384]{2,1,0:T(2,128)(2,1)S(1)}, u32[]{:S(2)}, u32[]{:S(2)}) async-start(bf16[8,2,16384]{2,1,0:T(2,128)(2,1)} %reshape.448), calls=%async_computation.4 | async-start | bytes 1048576 | tf_op jit(solution)/shard_map/all_to_all | solution.py:79
  85.4 26.6 %copy-start.7 = (bf16[1,128,256]{2,1,0:T(8,128)(2,1)}, bf16[1,128,256]{2,1,0:T(8,128)(2,1)S(1)}, u32[]{:S(2)}) copy-start(bf16[1,128,256]{2,1,0:T(8,128)(2,1)S(1)} %broadcast_select_fusion.4) | copy-start | bytes 196612
  85.4 13.6 %collective-permute-start.5 = (bf16[1,128,256]{2,1,0:T(8,128)(2,1)S(1)}, bf16[1,128,256]{2,1,0:T(8,128)(2,1)S(1)}, u32[]{:S(2)}, u32[]{:S(2)}) collective-permute-start(bf16[1,128,256]{2,1,0:T(8,128)(2,1)S(1)} %broadcast_select_fusion.4), channel_id=1, source_target_pairs={{8,0},{16,8},{24,16},{32,24},{40,32},{48,40},{56,48},{64,56},{72,6... | collective-permute-start | bytes 196616 | tf_op jit(solution)/shard_map/ppermute | solution.py:21
  87.3 9.7 %collective-permute-start.2 = (bf16[1,128,256]{2,1,0:T(8,128)(2,1)S(1)}, bf16[1,128,256]{2,1,0:T(8,128)(2,1)S(1)}, u32[]{:S(2)}, u32[]{:S(2)}) collective-permute-start(bf16[1,128,256]{2,1,0:T(8,128)(2,1)S(1)} %collective-permute-done), channel_id=1, source_target_pairs={{0,8},{8,16},{16,24},{24,32},{32,40},{40,48},{48,56},{56,64},{64,7... | collective-permute-start | bytes 196616 | tf_op jit(solution)/shard_map/ppermute | solution.py:18
  97.0 15.0 %copy-start.9 = (bf16[1,128,256]{2,1,0:T(8,128)(2,1)}, bf16[1,128,256]{2,1,0:T(8,128)(2,1)S(1)}, u32[]{:S(2)}) copy-start(bf16[1,128,256]{2,1,0:T(8,128)(2,1)S(1)} %collective-permute-done.2) | copy-start | bytes 196612
  97.0 29.0 %collective-permute-start.4 = (bf16[1,128,256]{2,1,0:T(8,128)(2,1)S(1)}, bf16[1,128,256]{2,1,0:T(8,128)(2,1)S(1)}, u32[]{:S(2)}, u32[]{:S(2)}) collective-permute-start(bf16[1,128,256]{2,1,0:T(8,128)(2,1)S(1)} %collective-permute-done.2), channel_id=1, source_target_pairs={{0,8},{8,16},{16,24},{24,32},{32,40},{40,48},{48,56},{56,64},{64,7... | collective-permute-start | bytes 196616 | tf_op jit(solution)/shard_map/ppermute | solution.py:18
  99.0 27.7 %copy-start.11 = (bf16[1,128,256]{2,1,0:T(8,128)(2,1)}, bf16[1,128,256]{2,1,0:T(8,128)(2,1)S(1)}, u32[]{:S(2)}) copy-start(bf16[1,128,256]{2,1,0:T(8,128)(2,1)S(1)} %broadcast_select_fusion.3) | copy-start | bytes 196612
  126.0 9.4 %copy-start.13 = (bf16[1,128,256]{2,1,0:T(8,128)(2,1)}, bf16[1,128,256]{2,1,0:T(8,128)(2,1)S(1)}, u32[]{:S(2)}) copy-start(bf16[1,128,256]{2,1,0:T(8,128)(2,1)S(1)} %collective-permute-done.4) | copy-start | bytes 196612
  126.7 9.7 %copy-start.17 = (pred[2,128,128]{1,2,0:T(8,128)(4,1)S(1)}, pred[2,128,128]{1,2,0:T(8,128)(4,1)}, u32[]{:S(2)}) copy-start(pred[2,128,128]{1,2,0:T(8,128)(4,1)} %get-tuple-element.37) | copy-start | bytes 98308
  128.0 15.2 %collective-permute-start.6 = (f32[1,128,256]{2,1,0:T(8,128)}, f32[1,128,256]{2,1,0:T(8,128)}, u32[]{:S(2)}, u32[]{:S(2)}) collective-permute-start(f32[1,128,256]{2,1,0:T(8,128)} %pad_maximum_fusion), channel_id=1, source_target_pairs={{8,0},{16,8},{24,16},{32,24},{40,32},{48,40},{56,48},{64,56},{72,6... | collective-permute-start | bytes 393224 | tf_op jit(solution)/shard_map/ppermute | solution.py:21
  135.8 1.4 copy-start.8
  135.8 1.4 copy-start.10
  135.8 1.4 copy-start.16
  136.1 1.0 copy-start.1
  137.1 1.4 copy-start.3
  137.5 2.2 %copy-start = (f32[2,8,128,128]{2,3,1,0:T(8,128)}, f32[2,8,128,128]{2,3,1,0:T(8,128)S(1)}, u32[]{:S(2)}) copy-start(f32[2,8,128,128]{2,3,1,0:T(8,128)S(1)} %fusion.19) | copy-start | bytes 3145732
  137.5 1.0 copy-start.12
  137.5 1.0 copy-start.14
  137.8 1.9 %copy-start.5 = (bf16[2,8,128,128]{2,3,1,0:T(8,128)(2,1)}, bf16[2,8,128,128]{2,3,1,0:T(8,128)(2,1)S(1)}, u32[]{:S(2)}) copy-start(bf16[2,8,128,128]{2,3,1,0:T(8,128)(2,1)S(1)} %fusion.33) | copy-start | bytes 1572868
  141.8 14.6 %copy-start.4 = (bf16[2,8,128,128]{2,3,1,0:T(8,128)(2,1)S(1)}, bf16[2,8,128,128]{2,3,1,0:T(8,128)(2,1)}, u32[]{:S(2)}) copy-start(bf16[2,8,128,128]{2,3,1,0:T(8,128)(2,1)} %copy-done.3) | copy-start | bytes 1572868
  143.2 30.3 %copy-start.2 = (bf16[2,8,128,128]{2,3,1,0:T(8,128)(2,1)S(1)}, bf16[2,8,128,128]{2,3,1,0:T(8,128)(2,1)}, u32[]{:S(2)}) copy-start(bf16[2,8,128,128]{2,3,1,0:T(8,128)(2,1)} %copy-done.1) | copy-start | bytes 1572868
  144.2 10.2 %collective-permute-start.7 = (f32[1,128,256]{2,1,0:T(8,128)S(1)}, f32[1,128,256]{2,1,0:T(8,128)S(1)}, u32[]{:S(2)}, u32[]{:S(2)}) collective-permute-start(f32[1,128,256]{2,1,0:T(8,128)S(1)} %get-tuple-element.23), channel_id=1, source_target_pairs={{0,8},{8,16},{16,24},{24,32},{32,40},{40,48},{48,56},{56,64},{64,7... | collective-permute-start | bytes 393224 | tf_op jit(solution)/shard_map/ppermute | solution.py:18
  154.4 6.9 %collective-permute-start.8 = (f32[1,128,256]{2,1,0:T(8,128)S(1)}, f32[1,128,256]{2,1,0:T(8,128)S(1)}, u32[]{:S(2)}, u32[]{:S(2)}) collective-permute-start(f32[1,128,256]{2,1,0:T(8,128)S(1)} %slice.81), channel_id=1, source_target_pairs={{8,0},{16,8},{24,16},{32,24},{40,32},{48,40},{56,48},{64,56},{72,6... | collective-permute-start | bytes 393224 | tf_op jit(solution)/shard_map/ppermute | solution.py:21
  161.3 10.2 %collective-permute-start.9 = (f32[1,128,256]{2,1,0:T(8,128)S(1)}, f32[1,128,256]{2,1,0:T(8,128)S(1)}, u32[]{:S(2)}, u32[]{:S(2)}) collective-permute-start(f32[1,128,256]{2,1,0:T(8,128)S(1)} %get-tuple-element.31), channel_id=1, source_target_pairs={{0,8},{8,16},{16,24},{24,32},{32,40},{40,48},{48,56},{56,64},{64,7... | collective-permute-start | bytes 393224 | tf_op jit(solution)/shard_map/ppermute | solution.py:18
  171.5 6.9 %collective-permute-start.10 = (f32[1,128,256]{2,1,0:T(8,128)S(1)}, f32[1,128,256]{2,1,0:T(8,128)S(1)}, u32[]{:S(2)}, u32[]{:S(2)}) collective-permute-start(f32[1,128,256]{2,1,0:T(8,128)S(1)} %slice.83), channel_id=1, source_target_pairs={{8,0},{16,8},{24,16},{32,24},{40,32},{48,40},{56,48},{64,56},{72,6... | collective-permute-start | bytes 393224 | tf_op jit(solution)/shard_map/ppermute | solution.py:21
  178.4 10.2 %collective-permute-start.11 = (f32[1,128,256]{2,1,0:T(8,128)S(1)}, f32[1,128,256]{2,1,0:T(8,128)S(1)}, u32[]{:S(2)}, u32[]{:S(2)}) collective-permute-start(f32[1,128,256]{2,1,0:T(8,128)S(1)} %get-tuple-element.29), channel_id=1, source_target_pairs={{0,8},{8,16},{16,24},{24,32},{32,40},{40,48},{48,56},{56,64},{64,7... | collective-permute-start | bytes 393224 | tf_op jit(solution)/shard_map/ppermute | solution.py:18
where the time goes:
time: 191 us; the launch traced here: 189 us
  starting transfers between devices  66.6 us (35%)
  local copies, waits for them, and re-layouts  65.8 us (34%)
  waiting for transfers between devices  39.5 us (21%)
  matrix products  9.39 us (5%)
  other arithmetic  6.6 us (3%)
    unnamed x59, local copies, waits for them, and re-layouts  44.3 us
    ppermute x6, starting transfers between devices, padded(): lax.ppermute(lax.slice_in_dim(block, 0, width, axis=dim), axis, backward)  26.7 us
    ppermute x6, waiting for transfers between devices, padded(): lax.ppermute(lax.slice_in_dim(block, block.shape[dim] - width, None, axis...  25.1 us
    ppermute x6, starting transfers between devices, padded(): lax.ppermute(lax.slice_in_dim(block, block.shape[dim] - width, None, axis...  13.5 us
    ppermute x6, waiting for transfers between devices, padded(): lax.ppermute(lax.slice_in_dim(block, 0, width, axis=dim), axis, backward)  9.24 us
    all_to_all x1, local copies, waits for them, and re-layouts, body(): lax.all_to_all(queries, 'kvh', split_axis=2, concat_axis=1, tiled=True)  8.9 us
    all_to_all x1, local copies, waits for them, and re-layouts, body(): lax.all_to_all(output_cotangent, 'kvh', split_axis=2, concat_axis=1, tile...  8.9 us
    all_to_all x1, starting transfers between devices, body(): lax.all_to_all(queries, 'kvh', split_axis=2, concat_axis=1, tiled=True)  4.82 us
  transfers between devices with their start and end apart: 18, of which 8 were waited for; matrix products, arithmetic and copies ran while one was open for 40% of the time, Pallas kernels for 0%

commit v1 on v0

v1 whole, which is shorter than its diff:
```python
import jax
import jax.numpy as jnp
from jax import lax
from jax.experimental import pallas as pl
from jax.experimental.pallas import tpu as pltpu
from jax.sharding import PartitionSpec as P

GROUP = 8
HEAD = 128
BLOCK = 128
DOCS = 64
INV_ROOT = HEAD**-0.5
LOG2E = 1.4426950408889634
MASKED = -1e30
BF = jnp.bfloat16
F32 = jnp.float32


def call(kernel, outs, n_in, smem=(), scratch=()):
    specs = [
        pl.BlockSpec(memory_space=pltpu.SMEM if i in smem else pltpu.VMEM) for i in range(n_in)
    ]
    return pl.pallas_call(
        kernel,
        out_shape=[jax.ShapeDtypeStruct(*o) for o in outs],
        in_specs=specs,
        out_specs=[pl.BlockSpec(memory_space=pltpu.VMEM)] * len(outs),
        scratch_shapes=list(scratch),
        compiler_params=pltpu.CompilerParams(vmem_limit_bytes=40 * 1024 * 1024),
    )


def two_terms(x):
    high = x.astype(BF)
    return high, (x - high.astype(F32)).astype(BF)


def pack_small(key_ref, value_ref, out_ref, grad_ref, norm_ref, packed_ref):
    heads = grad_ref.shape[2] // HEAD
    lane = lax.broadcasted_iota(jnp.int32, (16, heads), 1)
    for half in range(2):
        rows = pl.ds(half * 16, 16)
        delta = jnp.zeros((16, heads), F32)
        for n in range(heads):
            cols = pl.ds(n * HEAD, HEAD)
            product = out_ref[half, :, cols].astype(F32) * grad_ref[half, :, cols].astype(F32)
            delta = jnp.where(lane == n, jnp.sum(product, axis=1, keepdims=True), delta)
        stats = jnp.concatenate([*two_terms(norm_ref[half]), *two_terms(delta)], axis=1)
        for j in range(8):
            cols = pl.ds(j * HEAD, HEAD)
            packed_ref[j, rows, 0:128] = key_ref[half, :, cols]
            packed_ref[j, rows, 128:256] = value_ref[half, :, cols]
            packed_ref[j, rows, 256:512] = stats


def pack_large(query_ref, grad_ref, packed_ref):
    for half in range(2):
        rows = pl.ds(half * 16, 16)
        for j in range(8):
            cols = pl.ds(j * 1024, 1024)
            packed_ref[j, rows, 0:1024] = query_ref[half, :, cols]
            packed_ref[j, rows, 1024:2048] = grad_ref[half, :, cols]


def unpack_small(length_ref, packed_ref, low_ref, high_ref, stat_ref, start_ref, turned):
    ctx = lax.axis_index("ctx")
    kvh = lax.axis_index("kvh")
    for half, kv_ref in enumerate((low_ref, high_ref)):
        rows = pl.ds(half * 16, 16)
        kv_ref[...] = packed_ref[:, rows, 0:256].reshape(BLOCK, 256)
        stats = packed_ref[:, rows, 256:512].reshape(BLOCK, 256).astype(F32)
        turned[...] = stats.T
        first = pl.multiple_of(kvh * GROUP, GROUP)
        for s, factor in enumerate((LOG2E, 1.0)):
            total = (
                turned[pl.ds(s * 128 + first, GROUP), :]
                + turned[pl.ds(s * 128 + 64 + first, GROUP), :]
            )
            stat_ref[half, s] = total * factor
    row = lax.broadcasted_iota(jnp.int32, (8, BLOCK), 0)
    base = jnp.where(row == 0, ctx, 127 - ctx) * BLOCK
    position = base + lax.broadcasted_iota(jnp.int32, (8, BLOCK), 1)
    start = jnp.zeros((8, BLOCK), jnp.int32)
    end = jnp.int32(0)
    for j in range(DOCS):
        end = end + length_ref[j]
        start = jnp.where(position >= end, end, start)
    start_ref[...] = start - base


def pair_up(low_ref, high_ref, low1_ref, high1_ref, even_ref, odd_ref, pair1_ref):
    ctx = lax.axis_index("ctx")
    even = lax.rem(ctx, 2) == 0
    before_high = jnp.where(ctx == 63, low_ref[...], high1_ref[...])
    before_low = low1_ref[...]
    low, high = low_ref[...], high_ref[...]
    even_ref[0] = jnp.where(even, low, high)
    even_ref[1] = jnp.where(even, before_low, before_high)
    odd_ref[0] = jnp.where(even, high, low)
    odd_ref[1] = jnp.where(even, before_high, before_low)
    pair1_ref[0] = before_low
    pair1_ref[1] = before_high


def dot(a, b, contract):
    return lax.dot_general(a, b, ((contract[:1], contract[1:]), ((), ())), preferred_element_type=F32)


def gradients(
    rows_ref, low_ref, high_ref, pair1_ref, even_ref, odd_ref, stat_ref, start_ref,
    query_out, far_ref, near_ref, turned,
):
    ctx = lax.axis_index("ctx")
    even = lax.rem(ctx, 2) == 0
    key_at = lax.broadcasted_iota(jnp.int32, (BLOCK, BLOCK), 0)
    row_at = lax.broadcasted_iota(jnp.int32, (BLOCK, BLOCK), 1)
    for half, own_ref in enumerate((low_ref, high_ref)):
        start = start_ref[half : half + 1, :]
        takes_even = even if half == 0 else jnp.logical_not(even)
        for far in (True, False):
            if far:
                tiles = [jnp.where(takes_even, even_ref[s], odd_ref[s]) for s in range(2)]
            else:
                tiles = [own_ref[...], pair1_ref[half]]
            allowed = [key_at - BLOCK * (s + 2 * far) >= start for s in range(2)]
            if not far:
                allowed[0] = allowed[0] & (key_at <= row_at)
            bias = jnp.concatenate([jnp.where(a, 0.0, MASKED) for a in allowed], axis=0)
            bias = jnp.concatenate([bias, bias], axis=1)
            keys = jnp.concatenate([t[:, :HEAD] for t in tiles], axis=0)
            values = jnp.concatenate([t[:, HEAD:] for t in tiles], axis=0)
            keys_turned = keys.T
            key_total = jnp.zeros((2 * BLOCK, HEAD), F32)
            value_total = jnp.zeros((2 * BLOCK, HEAD), F32)
            for g in range(0, GROUP, 2):
                def head_pair(offset):
                    return jnp.concatenate(
                        [
                            rows_ref[
                                :, half * 16 : half * 16 + 16,
                                offset + n * HEAD : offset + (n + 1) * HEAD,
                            ].reshape(BLOCK, HEAD)
                            for n in (g, g + 1)
                        ],
                        axis=0,
                    )

                query, grad = head_pair(0), head_pair(1024)
                norm, delta = (
                    jnp.concatenate([stat_ref[half, s, n : n + 1, :] for n in (g, g + 1)], axis=1)
                    for s in range(2)
                )
                scores = dot(keys, query, (1, 1))
                weights = jnp.exp2(scores * (INV_ROOT * LOG2E) - norm + bias)
                weight_grad = dot(values, grad, (1, 1))
                score_grad = (weights * (weight_grad - delta)).astype(BF)
                value_total += dot(weights.astype(BF), grad, (1, 0))
                key_total += dot(score_grad, query, (1, 0))
                query_part = dot(keys_turned, score_grad, (1, 0))
                if far:
                    turned[:, g * HEAD : (g + 2) * HEAD] = query_part
                else:
                    query_part = (query_part + turned[:, g * HEAD : (g + 2) * HEAD]) * INV_ROOT
                    for n in range(2):
                        query_out[half, :, (g + n) * HEAD : (g + n + 1) * HEAD] = (
                            query_part[:, n * HEAD : (n + 1) * HEAD].T.astype(BF)
                        )
            key_total = key_total * INV_ROOT
            if far:
                slot = jnp.where(takes_even, 0, 1)
                for s in range(2):
                    part = slice(s * BLOCK, (s + 1) * BLOCK)
                    far_ref[slot, s, :, :HEAD] = key_total[part].astype(BF)
                    far_ref[slot, s, :, HEAD:] = value_total[part].astype(BF)
            else:
                for s in range(2):
                    part = slice(s * BLOCK, (s + 1) * BLOCK)
                    near_ref[half, s, :, :HEAD] = key_total[part]
                    near_ref[half, s, :, HEAD:] = value_total[part]


def add_far(near_ref, even_ref, odd_ref, own_ref, low_ref, high_ref, fold_ref):
    even = lax.rem(lax.axis_index("ctx"), 2) == 0
    for half, send_ref in enumerate((low_ref, high_ref)):
        takes_even = even if half == 0 else jnp.logical_not(even)
        got = [
            jnp.where(takes_even, even_ref[s].astype(F32), odd_ref[s].astype(F32)) for s in range(2)
        ]
        own_ref[half] = near_ref[half, 0] + got[0]
        before = near_ref[half, 1] + got[1]
        send_ref[...] = before.astype(BF)
        if half == 1:
            fold_ref[...] = before


def add_near(own_ref, fold_ref, low_ref, high_ref, key_out, value_out):
    at_fold = lax.axis_index("ctx") == 63
    for half, got_ref in enumerate((low_ref, high_ref)):
        got = got_ref[...].astype(F32)
        if half == 0:
            got = jnp.where(at_fold, fold_ref[...], got)
        total = own_ref[half] + got
        key_out[half] = total[:, :HEAD].astype(BF)
        value_out[half] = total[:, HEAD:].astype(BF)


def body(lengths, queries, keys, values, outputs, grads, norms):
    last = 2 * lax.axis_size("ctx") - 1

    def owner(p):
        return min(p, last - p)

    up = [(i, i + 1) for i in range(last // 2)]
    down = [(j, i) for i, j in up]
    skips = [[(owner(p), owner(p + 2)) for p in range(first, last - 1, 2)] for first in range(2)]
    backs = [[(j, i) for i, j in skip] for skip in skips]

    def by_head(x):
        return lax.all_to_all(x, "kvh", split_axis=0, concat_axis=0, tiled=True)

    (small,) = call(pack_small, [((8, 32, 512), BF)], 5)(keys, values, outputs, grads, norms)
    small = by_head(small)
    (large,) = call(pack_large, [((8, 32, 2048), BF)], 2)(queries, grads)
    large = by_head(large)
    tile, pair = ((BLOCK, 256), BF), ((2, BLOCK, 256), BF)
    low, high, stats, starts = call(
        unpack_small,
        [tile, tile, ((2, 2, GROUP, BLOCK), F32), ((8, BLOCK), jnp.int32)],
        2,
        smem=(0,),
        scratch=[pltpu.VMEM((256, BLOCK), F32)],
    )(lengths, small)
    low1 = lax.ppermute(low, "ctx", up)
    high1 = lax.ppermute(high, "ctx", down)
    even, odd, pair1 = call(pair_up, [pair, pair, pair], 4)(low, high, low1, high1)
    even, odd = (lax.ppermute(x, "ctx", skip) for x, skip in zip((even, odd), skips))
    query_grad, far, near = call(
        gradients,
        [
            ((2, BLOCK, 1024), BF),
            ((2, 2, BLOCK, 256), BF),
            ((2, 2, BLOCK, 256), F32),
        ],
        8,
        scratch=[pltpu.VMEM((HEAD, 1024), F32)],
    )(large, low, high, pair1, even, odd, stats, starts)
    even, odd = (lax.ppermute(far[s], "ctx", backs[s]) for s in range(2))
    own, low, high, fold = call(
        add_far, [((2, BLOCK, 256), F32), tile, tile, ((BLOCK, 256), F32)], 3
    )(near, even, odd)
    low = lax.ppermute(low, "ctx", down)
    high = lax.ppermute(high, "ctx", up)
    key_grad, value_grad = call(add_near, [((2, BLOCK, HEAD), BF)] * 2, 4)(own, fold, low, high)
    return query_grad, key_grad, value_grad


def solution(mesh):
    rows = P(None, ("ctx", "kvh"), None)
    heads = P(None, "ctx", "kvh")
    return jax.shard_map(
        body,
        mesh=mesh,
        in_specs=(P(),) + (rows,) * 6,
        out_specs=(heads,) * 3,
        check_vma=False,
    )
```

time: 191 us -> 82.9 us (0.43)
  the two profiles are of different devices: /device:TPU:384 before, /device:TPU:424 now
where the time goes in v1:
time: 82.9 us; the launch traced here: 82.3 us
  starting transfers between devices  46.3 us (56%)
  waiting for transfers between devices  22.1 us (27%)
  Pallas kernels  8.52 us (10%)
  local copies, waits for them, and re-layouts  4.5 us (5%)
    ppermute x1, starting transfers between devices, body(): low = lax.ppermute(low, 'ctx', down)  10 us
    all_to_all x2, starting transfers between devices, by_head(): return lax.all_to_all(x, 'kvh', split_axis=0, concat_axis=0, tiled=True)  9.97 us
    ppermute x2, starting transfers between devices, body(): even, odd = (lax.ppermute(far[s], 'ctx', backs[s]) for s in range(2))  8.25 us
    ppermute x2, starting transfers between devices, body(): lax.ppermute(x, 'ctx', skip)  8.25 us
    ppermute x1, waiting for transfers between devices, body(): high = lax.ppermute(high, 'ctx', up)  6.33 us
    all_to_all x2, waiting for transfers between devices, by_head(): return lax.all_to_all(x, 'kvh', split_axis=0, concat_axis=0, tiled=True)  5 us
    pallas_call x1, Pallas kernels, body(): call(gradients, [((2, BLOCK, 1024), BF), ((2, 2, BLOCK, 256), BF), ((2, 2...  4.76 us
    ppermute x1, starting transfers between devices, body(): high1 = lax.ppermute(high, 'ctx', down)  4.55 us
  transfers between devices with their start and end apart: 10, of which 8 were waited for; matrix products, arithmetic and copies ran while one was open for 0% of the time, Pallas kernels for 2%

profile of v1, /device:TPU:424, one launch (start us, length us, event | category | flops | bytes accessed | tf_op | source)
XLA Modules:
  0.0 82.3 jit_solution(5819103820011906107)
XLA Ops:
  0.6 0.0 copy-start
  0.6 1.0 %copy-done = bf16[2,16,8192]{2,1,0:T(8,128)(2,1)S(1)} copy-done((bf16[2,16,8192]{2,1,0:T(8,128)(2,1)S(1)}, bf16[2,16,8192]{2,1,0:T(8,128)(2,1)}, u32[]{:S(2)}) %copy-start) | copy-done | bytes 524312
  1.7 0.0 copy-start.2
  1.7 1.0 %copy-done.2 = bf16[2,16,8192]{2,1,0:T(8,128)(2,1)S(1)} copy-done((bf16[2,16,8192]{2,1,0:T(8,128)(2,1)S(1)}, bf16[2,16,8192]{2,1,0:T(8,128)(2,1)}, u32[]{:S(2)}) %copy-start.2) | copy-done | bytes 524312
  2.7 0.0 copy-start.4
  2.7 0.8 %copy-done.4 = bf16[2,16,1024]{2,1,0:T(8,128)(2,1)S(1)} copy-done((bf16[2,16,1024]{2,1,0:T(8,128)(2,1)S(1)}, bf16[2,16,1024]{2,1,0:T(8,128)(2,1)}, u32[]{:S(2)}) %copy-start.4) | copy-done | bytes 65560
  3.6 0.0 copy-start.5
  3.6 0.8 %copy-done.5 = bf16[2,16,1024]{2,1,0:T(8,128)(2,1)S(1)} copy-done((bf16[2,16,1024]{2,1,0:T(8,128)(2,1)S(1)}, bf16[2,16,1024]{2,1,0:T(8,128)(2,1)}, u32[]{:S(2)}) %copy-start.5) | copy-done | bytes 65560
  4.4 0.0 copy-start.6
  4.4 0.7 copy-done.6
  5.1 0.0 copy-start.3
  5.1 1.2 %shard_map.95 = bf16[8,32,512]{2,1,0:T(8,128)(2,1)} custom-call(bf16[2,16,1024]{2,1,0:T(8,128)(2,1)S(1)} %copy-done.4, bf16[2,16,1024]{2,1,0:T(8,128)(2,1)S(1)} %copy-done.5, bf16[2,16,8192]{2,1,0:T(8,128)(2,1)S(1)} %copy-done.2, bf16[2,16,8192]{2,1,0:T(8,128)(2,1)S(1)} %copy-done, f32[2,16,64]{2,1,0:T(8,128)S(1)} %copy-done.6), custom_call_target="tpu_custom_call" | custom-call | tf_op jit(solution)/shard_map/pallas_call | solution.py:221
  6.3 0.0 copy-start.1
  6.3 5.0 %all-to-all-start.1 = ((bf16[8,32,512]{2,1,0:T(8,128)(2,1)}), bf16[8,32,512]{2,1,0:T(8,128)(2,1)S(1)}, u32[]{:S(2)}, u32[]{:S(2)}) async-start(bf16[8,32,512]{2,1,0:T(8,128)(2,1)} %shard_map.95), calls=%async_computation.1 | async-start | bytes 524288 | tf_op jit(solution)/shard_map/all_to_all | solution.py:219
  11.4 0.0 copy-done.3
  11.4 0.0 copy-done.1
  11.4 1.1 %shard_map.94 = bf16[8,32,2048]{2,1,0:T(8,128)(2,1)} custom-call(bf16[2,16,8192]{2,1,0:T(8,128)(2,1)S(1)} %copy-done.3, bf16[2,16,8192]{2,1,0:T(8,128)(2,1)S(1)} %copy-done.1), custom_call_target="tpu_custom_call" | custom-call | tf_op jit(solution)/shard_map/pallas_call | solution.py:223
  12.5 0.0 copy-start.7
  12.5 5.0 %all-to-all-done.1.packed_ref = bf16[8,32,512]{2,1,0:T(8,128)(2,1)S(1)} async-done(((bf16[8,32,512]{2,1,0:T(8,128)(2,1)}), bf16[8,32,512]{2,1,0:T(8,128)(2,1)S(1)}, u32[]{:S(2)}, u32[]{:S(2)}) %all-to-all-start.1) | async-done | bytes 262176 | tf_op jit(solution)/shard_map/all_to_all | solution.py:219
  17.5 4.9 %all-to-all-start = ((bf16[8,32,2048]{2,1,0:T(8,128)(2,1)}), bf16[8,32,2048]{2,1,0:T(8,128)(2,1)S(1)}, u32[]{:S(2)}, u32[]{:S(2)}) async-start(bf16[8,32,2048]{2,1,0:T(8,128)(2,1)} %shard_map.94), calls=%async_computation | async-start | bytes 2097152 | tf_op jit(solution)/shard_map/all_to_all | solution.py:219
  22.4 0.0 copy-done.7
  22.4 0.7 shard_map.96
  23.1 3.4 %collective-permute-start = (bf16[128,256]{1,0:T(8,128)(2,1)S(1)}, bf16[128,256]{1,0:T(8,128)(2,1)S(1)}, u32[]{:S(2)}, u32[]{:S(2)}) collective-permute-start(bf16[128,256]{1,0:T(8,128)(2,1)S(1)} %get-tuple-element.19.low_ref), channel_id=1, source_target_pairs={{0,8},{8,16},{16,24},{24,32},{32,40},{40,48},{48,56},{56,64},{64,7... | collective-permute-start | bytes 196616 | tf_op jit(solution)/shard_map/ppermute | solution.py:233
  26.5 4.6 %collective-permute-start.1 = (bf16[128,256]{1,0:T(8,128)(2,1)S(1)}, bf16[128,256]{1,0:T(8,128)(2,1)S(1)}, u32[]{:S(2)}, u32[]{:S(2)}) collective-permute-start(bf16[128,256]{1,0:T(8,128)(2,1)S(1)} %get-tuple-element.20.high_ref), channel_id=1, source_target_pairs={{8,0},{16,8},{24,16},{32,24},{40,32},{48,40},{56,48},{64,56},{72,6... | collective-permute-start | bytes 196616 | tf_op jit(solution)/shard_map/ppermute | solution.py:234
  31.0 0.3 collective-permute-done.low1_ref
  31.3 1.6 %collective-permute-done.1.high1_ref = bf16[128,256]{1,0:T(8,128)(2,1)S(1)} collective-permute-done((bf16[128,256]{1,0:T(8,128)(2,1)S(1)}, bf16[128,256]{1,0:T(8,128)(2,1)S(1)}, u32[]{:S(2)}, u32[]{:S(2)}) %collective-permute-start.1) | collective-permute-done | bytes 65568 | tf_op jit(solution)/shard_map/ppermute | solution.py:234
  33.0 4.4 %collective-permute-start.2 = (bf16[2,128,256]{2,1,0:T(8,128)(2,1)S(1)}, bf16[2,128,256]{2,1,0:T(8,128)(2,1)S(1)}, u32[]{:S(2)}, u32[]{:S(2)}) collective-permute-start(bf16[2,128,256]{2,1,0:T(8,128)(2,1)S(1)} %get-tuple-element.22), channel_id=1, source_target_pairs={{0,16},{16,32},{32,48},{48,64},{64,80},{80,96},{96,112},{112,128},... | collective-permute-start | bytes 393224 | tf_op jit(solution)/shard_map/ppermute | solution.py:236
  37.3 3.9 %collective-permute-start.3 = (bf16[2,128,256]{2,1,0:T(8,128)(2,1)S(1)}, bf16[2,128,256]{2,1,0:T(8,128)(2,1)S(1)}, u32[]{:S(2)}, u32[]{:S(2)}) collective-permute-start(bf16[2,128,256]{2,1,0:T(8,128)(2,1)S(1)} %get-tuple-element.23), channel_id=1, source_target_pairs={{8,24},{24,40},{40,56},{56,72},{72,88},{88,104},{104,120},{120,136... | collective-permute-start | bytes 393224 | tf_op jit(solution)/shard_map/ppermute | solution.py:236
  41.2 1.0 %collective-permute-done.2.even_ref = bf16[2,128,256]{2,1,0:T(8,128)(2,1)S(1)} collective-permute-done((bf16[2,128,256]{2,1,0:T(8,128)(2,1)S(1)}, bf16[2,128,256]{2,1,0:T(8,128)(2,1)S(1)}, u32[]{:S(2)}, u32[]{:S(2)}) %collective-permute-start.2) | collective-permute-done | bytes 131104 | tf_op jit(solution)/shard_map/ppermute | solution.py:236
  42.2 3.4 %collective-permute-done.3.odd_ref = bf16[2,128,256]{2,1,0:T(8,128)(2,1)S(1)} collective-permute-done((bf16[2,128,256]{2,1,0:T(8,128)(2,1)S(1)}, bf16[2,128,256]{2,1,0:T(8,128)(2,1)S(1)}, u32[]{:S(2)}, u32[]{:S(2)}) %collective-permute-start.3) | collective-permute-done | bytes 131104 | tf_op jit(solution)/shard_map/ppermute | solution.py:236
  45.7 0.0 all-to-all-done.rows_ref
  45.7 4.8 %shard_map.98 = (bf16[2,128,1024]{2,1,0:T(8,128)(2,1)}, bf16[2,2,128,256]{3,2,1,0:T(8,128)(2,1)S(1)}, f32[2,2,128,256]{3,2,1,0:T(8,128)S(1)}) custom-call(bf16[8,32,2048]{2,1,0:T(8,128)(2,1)S(1)} %all-to-all-done.rows_ref, bf16[128,256]{1,0:T(8,128)(2,1)S(1)} %get-tuple-element.19.low_ref, bf16[128,256]{1,0:T(8,128)(2,1)S(1)} %get-tuple-element.20.high_ref, ...), custom_call_target="tpu_custom_call" | custom-call | tf_op jit(solution)/shard_map/pallas_call | solution.py:237
  50.5 4.3 %collective-permute-start.5 = (bf16[2,128,256]{2,1,0:T(8,128)(2,1)S(1)}, bf16[2,128,256]{2,1,0:T(8,128)(2,1)S(1)}, u32[]{:S(2)}, u32[]{:S(2)}) collective-permute-start(bf16[2,128,256]{2,1,0:T(8,128)(2,1)S(1)} %get-tuple-element.35), channel_id=1, source_target_pairs={{24,8},{40,24},{56,40},{72,56},{88,72},{104,88},{120,104},{136,120... | collective-permute-start | bytes 393224 | tf_op jit(solution)/shard_map/ppermute | solution.py:247
  54.8 3.9 %collective-permute-start.4 = (bf16[2,128,256]{2,1,0:T(8,128)(2,1)S(1)}, bf16[2,128,256]{2,1,0:T(8,128)(2,1)S(1)}, u32[]{:S(2)}, u32[]{:S(2)}) collective-permute-start(bf16[2,128,256]{2,1,0:T(8,128)(2,1)S(1)} %get-tuple-element.36), channel_id=1, source_target_pairs={{16,0},{32,16},{48,32},{64,48},{80,64},{96,80},{112,96},{128,112},... | collective-permute-start | bytes 393224 | tf_op jit(solution)/shard_map/ppermute | solution.py:247
  58.7 1.1 %collective-permute-done.5.odd_ref = bf16[2,128,256]{2,1,0:T(8,128)(2,1)S(1)} collective-permute-done((bf16[2,128,256]{2,1,0:T(8,128)(2,1)S(1)}, bf16[2,128,256]{2,1,0:T(8,128)(2,1)S(1)}, u32[]{:S(2)}, u32[]{:S(2)}) %collective-permute-start.5) | collective-permute-done | bytes 131104 | tf_op jit(solution)/shard_map/ppermute | solution.py:247
  59.8 3.4 %collective-permute-done.4.even_ref = bf16[2,128,256]{2,1,0:T(8,128)(2,1)S(1)} collective-permute-done((bf16[2,128,256]{2,1,0:T(8,128)(2,1)S(1)}, bf16[2,128,256]{2,1,0:T(8,128)(2,1)S(1)}, u32[]{:S(2)}, u32[]{:S(2)}) %collective-permute-start.4) | collective-permute-done | bytes 131104 | tf_op jit(solution)/shard_map/ppermute | solution.py:247
  63.2 0.1 shard_map.99
  63.3 10.0 %collective-permute-start.6 = (bf16[128,256]{1,0:T(8,128)(2,1)S(1)}, bf16[128,256]{1,0:T(8,128)(2,1)S(1)}, u32[]{:S(2)}, u32[]{:S(2)}) collective-permute-start(bf16[128,256]{1,0:T(8,128)(2,1)S(1)} %get-tuple-element.31), channel_id=1, source_target_pairs={{8,0},{16,8},{24,16},{32,24},{40,32},{48,40},{56,48},{64,56},{72,6... | collective-permute-start | bytes 196616 | tf_op jit(solution)/shard_map/ppermute | solution.py:251
  73.3 1.9 %collective-permute-start.7 = (bf16[128,256]{1,0:T(8,128)(2,1)S(1)}, bf16[128,256]{1,0:T(8,128)(2,1)S(1)}, u32[]{:S(2)}, u32[]{:S(2)}) collective-permute-start(bf16[128,256]{1,0:T(8,128)(2,1)S(1)} %get-tuple-element.32), channel_id=1, source_target_pairs={{0,8},{8,16},{16,24},{24,32},{32,40},{40,48},{48,56},{56,64},{64,7... | collective-permute-start | bytes 196616 | tf_op jit(solution)/shard_map/ppermute | solution.py:252
  75.2 0.0 collective-permute-done.6.low_ref
  75.2 6.3 %collective-permute-done.7.high_ref = bf16[128,256]{1,0:T(8,128)(2,1)S(1)} collective-permute-done((bf16[128,256]{1,0:T(8,128)(2,1)S(1)}, bf16[128,256]{1,0:T(8,128)(2,1)S(1)}, u32[]{:S(2)}, u32[]{:S(2)}) %collective-permute-start.7) | collective-permute-done | bytes 65568 | tf_op jit(solution)/shard_map/ppermute | solution.py:252
  81.6 0.7 shard_map.100
  (2 shorter events, 0.1 us)
Async XLA Ops:
  0.6 1.0 %copy-start = (bf16[2,16,8192]{2,1,0:T(8,128)(2,1)S(1)}, bf16[2,16,8192]{2,1,0:T(8,128)(2,1)}, u32[]{:S(2)}) copy-start(bf16[2,16,8192]{2,1,0:T(8,128)(2,1)} %grad_ref.3) | copy-start | bytes 1572868
  1.7 1.0 %copy-start.2 = (bf16[2,16,8192]{2,1,0:T(8,128)(2,1)S(1)}, bf16[2,16,8192]{2,1,0:T(8,128)(2,1)}, u32[]{:S(2)}) copy-start(bf16[2,16,8192]{2,1,0:T(8,128)(2,1)} %out_ref.1) | copy-start | bytes 1572868
  2.7 0.8 %copy-start.4 = (bf16[2,16,1024]{2,1,0:T(8,128)(2,1)S(1)}, bf16[2,16,1024]{2,1,0:T(8,128)(2,1)}, u32[]{:S(2)}) copy-start(bf16[2,16,1024]{2,1,0:T(8,128)(2,1)} %key_ref.1) | copy-start | bytes 196612
  3.6 0.8 %copy-start.5 = (bf16[2,16,1024]{2,1,0:T(8,128)(2,1)S(1)}, bf16[2,16,1024]{2,1,0:T(8,128)(2,1)}, u32[]{:S(2)}) copy-start(bf16[2,16,1024]{2,1,0:T(8,128)(2,1)} %value_ref.1) | copy-start | bytes 196612
  4.4 0.7 copy-start.6
  5.1 6.3 %copy-start.3 = (bf16[2,16,8192]{2,1,0:T(8,128)(2,1)S(1)}, bf16[2,16,8192]{2,1,0:T(8,128)(2,1)}, u32[]{:S(2)}) copy-start(bf16[2,16,8192]{2,1,0:T(8,128)(2,1)} %query_ref.1) | copy-start | bytes 1572868
  6.3 5.1 %copy-start.1 = (bf16[2,16,8192]{2,1,0:T(8,128)(2,1)S(1)}, bf16[2,16,8192]{2,1,0:T(8,128)(2,1)}, u32[]{:S(2)}) copy-start(bf16[2,16,8192]{2,1,0:T(8,128)(2,1)} %grad_ref.3) | copy-start | bytes 1572868
  6.3 11.1 %all-to-all-start.1 = ((bf16[8,32,512]{2,1,0:T(8,128)(2,1)}), bf16[8,32,512]{2,1,0:T(8,128)(2,1)S(1)}, u32[]{:S(2)}, u32[]{:S(2)}) async-start(bf16[8,32,512]{2,1,0:T(8,128)(2,1)} %shard_map.95), calls=%async_computation.1 | async-start | bytes 524288 | tf_op jit(solution)/shard_map/all_to_all | solution.py:219
  12.5 9.9 %copy-start.7 = (s32[64]{0:T(128)S(1)}, s32[64]{0:T(128)}, u32[]{:S(2)}) copy-start(s32[64]{0:T(128)} %length_ref.1) | copy-start | bytes 772
  17.5 28.2 %all-to-all-start = ((bf16[8,32,2048]{2,1,0:T(8,128)(2,1)}), bf16[8,32,2048]{2,1,0:T(8,128)(2,1)S(1)}, u32[]{:S(2)}, u32[]{:S(2)}) async-start(bf16[8,32,2048]{2,1,0:T(8,128)(2,1)} %shard_map.94), calls=%async_computation | async-start | bytes 2097152 | tf_op jit(solution)/shard_map/all_to_all | solution.py:219
  23.1 8.3 %collective-permute-start = (bf16[128,256]{1,0:T(8,128)(2,1)S(1)}, bf16[128,256]{1,0:T(8,128)(2,1)S(1)}, u32[]{:S(2)}, u32[]{:S(2)}) collective-permute-start(bf16[128,256]{1,0:T(8,128)(2,1)S(1)} %get-tuple-element.19.low_ref), channel_id=1, source_target_pairs={{0,8},{8,16},{16,24},{24,32},{32,40},{40,48},{48,56},{56,64},{64,7... | collective-permute-start | bytes 196616 | tf_op jit(solution)/shard_map/ppermute | solution.py:233
  26.5 6.4 %collective-permute-start.1 = (bf16[128,256]{1,0:T(8,128)(2,1)S(1)}, bf16[128,256]{1,0:T(8,128)(2,1)S(1)}, u32[]{:S(2)}, u32[]{:S(2)}) collective-permute-start(bf16[128,256]{1,0:T(8,128)(2,1)S(1)} %get-tuple-element.20.high_ref), channel_id=1, source_target_pairs={{8,0},{16,8},{24,16},{32,24},{40,32},{48,40},{56,48},{64,56},{72,6... | collective-permute-start | bytes 196616 | tf_op jit(solution)/shard_map/ppermute | solution.py:234
  33.0 9.3 %collective-permute-start.2 = (bf16[2,128,256]{2,1,0:T(8,128)(2,1)S(1)}, bf16[2,128,256]{2,1,0:T(8,128)(2,1)S(1)}, u32[]{:S(2)}, u32[]{:S(2)}) collective-permute-start(bf16[2,128,256]{2,1,0:T(8,128)(2,1)S(1)} %get-tuple-element.22), channel_id=1, source_target_pairs={{0,16},{16,32},{32,48},{48,64},{64,80},{80,96},{96,112},{112,128},... | collective-permute-start | bytes 393224 | tf_op jit(solution)/shard_map/ppermute | solution.py:236
  37.3 8.4 %collective-permute-start.3 = (bf16[2,128,256]{2,1,0:T(8,128)(2,1)S(1)}, bf16[2,128,256]{2,1,0:T(8,128)(2,1)S(1)}, u32[]{:S(2)}, u32[]{:S(2)}) collective-permute-start(bf16[2,128,256]{2,1,0:T(8,128)(2,1)S(1)} %get-tuple-element.23), channel_id=1, source_target_pairs={{8,24},{24,40},{40,56},{56,72},{72,88},{88,104},{104,120},{120,136... | collective-permute-start | bytes 393224 | tf_op jit(solution)/shard_map/ppermute | solution.py:236
  50.5 9.4 %collective-permute-start.5 = (bf16[2,128,256]{2,1,0:T(8,128)(2,1)S(1)}, bf16[2,128,256]{2,1,0:T(8,128)(2,1)S(1)}, u32[]{:S(2)}, u32[]{:S(2)}) collective-permute-start(bf16[2,128,256]{2,1,0:T(8,128)(2,1)S(1)} %get-tuple-element.35), channel_id=1, source_target_pairs={{24,8},{40,24},{56,40},{72,56},{88,72},{104,88},{120,104},{136,120... | collective-permute-start | bytes 393224 | tf_op jit(solution)/shard_map/ppermute | solution.py:247
  54.8 8.4 %collective-permute-start.4 = (bf16[2,128,256]{2,1,0:T(8,128)(2,1)S(1)}, bf16[2,128,256]{2,1,0:T(8,128)(2,1)S(1)}, u32[]{:S(2)}, u32[]{:S(2)}) collective-permute-start(bf16[2,128,256]{2,1,0:T(8,128)(2,1)S(1)} %get-tuple-element.36), channel_id=1, source_target_pairs={{16,0},{32,16},{48,32},{64,48},{80,64},{96,80},{112,96},{128,112},... | collective-permute-start | bytes 393224 | tf_op jit(solution)/shard_map/ppermute | solution.py:247
  63.3 11.9 %collective-permute-start.6 = (bf16[128,256]{1,0:T(8,128)(2,1)S(1)}, bf16[128,256]{1,0:T(8,128)(2,1)S(1)}, u32[]{:S(2)}, u32[]{:S(2)}) collective-permute-start(bf16[128,256]{1,0:T(8,128)(2,1)S(1)} %get-tuple-element.31), channel_id=1, source_target_pairs={{8,0},{16,8},{24,16},{32,24},{40,32},{48,40},{56,48},{64,56},{72,6... | collective-permute-start | bytes 196616 | tf_op jit(solution)/shard_map/ppermute | solution.py:251
  73.3 8.3 %collective-permute-start.7 = (bf16[128,256]{1,0:T(8,128)(2,1)S(1)}, bf16[128,256]{1,0:T(8,128)(2,1)S(1)}, u32[]{:S(2)}, u32[]{:S(2)}) collective-permute-start(bf16[128,256]{1,0:T(8,128)(2,1)S(1)} %get-tuple-element.32), channel_id=1, source_target_pairs={{0,8},{8,16},{16,24},{24,32},{32,40},{40,48},{48,56},{56,64},{64,7... | collective-permute-start | bytes 196616 | tf_op jit(solution)/shard_map/ppermute | solution.py:252

commit v2 on v1

v2 whole, which is shorter than its diff:
```python
import jax
import jax.numpy as jnp
from jax import lax
from jax.experimental import pallas as pl
from jax.experimental.pallas import tpu as pltpu
from jax.sharding import PartitionSpec as P

GROUP = 8
HEAD = 128
BLOCK = 128
DOCS = 64
INV_ROOT = HEAD**-0.5
LOG2E = 1.4426950408889634
MASKED = -1e30
ALL = 60
BF = jnp.bfloat16
F32 = jnp.float32


def call(kernel, outs, n_in, smem=(), scratch=(), raw=False):
    place = pltpu.HBM if raw else pltpu.VMEM
    specs = [pl.BlockSpec(memory_space=pltpu.SMEM if i in smem else place) for i in range(n_in)]
    return pl.pallas_call(
        kernel,
        out_shape=[jax.ShapeDtypeStruct(*o) for o in outs],
        in_specs=specs,
        out_specs=[pl.BlockSpec(memory_space=pltpu.VMEM)] * len(outs),
        scratch_shapes=list(scratch),
        compiler_params=pltpu.CompilerParams(vmem_limit_bytes=(ALL if raw else 40) * 1024 * 1024),
    )


def fetch(sources, targets, sems):
    copies = [
        pltpu.make_async_copy(source, target, sems.at[i])
        for i, (source, target) in enumerate(zip(sources, targets))
    ]
    for copy in copies:
        copy.start()
    for copy in copies:
        copy.wait()


def two_terms(x):
    high = x.astype(BF)
    return high, (x - high.astype(F32)).astype(BF)


def pack_small(key_raw, value_raw, packed_ref, key_ref, value_ref, sems):
    fetch((key_raw, value_raw), (key_ref, value_ref), sems)
    for half in range(2):
        rows = pl.ds(half * 16, 16)
        for j in range(8):
            cols = pl.ds(j * HEAD, HEAD)
            packed_ref[j, rows, :HEAD] = key_ref[half, :, cols]
            packed_ref[j, rows, HEAD:] = value_ref[half, :, cols]


def pack_large(length_ref, *refs):
    packed_ref, start_ref, sems = refs[4], refs[5], refs[10]
    fetch(refs[:4], refs[6:10], sems)
    query_ref, grad_ref, out_ref, norm_ref = refs[6:10]
    heads = grad_ref.shape[2] // HEAD
    lane = lax.broadcasted_iota(jnp.int32, (16, heads), 1)
    source = lax.broadcasted_iota(jnp.int32, (4 * heads, HEAD), 0)
    target = lax.broadcasted_iota(jnp.int32, (4 * heads, HEAD), 1)
    offset = source - (lax.div(target, GROUP) * heads + lax.rem(target, GROUP))
    stats = []
    for half in range(2):
        delta = jnp.zeros((16, heads), F32)
        for n in range(heads):
            cols = pl.ds(n * HEAD, HEAD)
            product = out_ref[half, :, cols].astype(F32) * grad_ref[half, :, cols].astype(F32)
            delta = jnp.where(lane == n, jnp.sum(product, axis=1, keepdims=True), delta)
        stats.append(jnp.concatenate([*two_terms(norm_ref[half]), *two_terms(delta)], axis=1))
    stats = jnp.concatenate(stats, axis=0)
    for j in range(8):
        pick = jnp.where((offset == j * GROUP) & (target < 4 * GROUP), 1.0, 0.0).astype(BF)
        packed_ref[j, :, 2048:] = dot(stats, pick, (1, 0)).astype(BF)
        for half in range(2):
            rows = pl.ds(half * 16, 16)
            cols = pl.ds(j * 1024, 1024)
            packed_ref[j, rows, 0:1024] = query_ref[half, :, cols]
            packed_ref[j, rows, 1024:2048] = grad_ref[half, :, cols]
    ctx = lax.axis_index("ctx")
    row = lax.broadcasted_iota(jnp.int32, (8, BLOCK), 0)
    base = jnp.where(row == 0, ctx, 127 - ctx) * BLOCK
    position = base + lax.broadcasted_iota(jnp.int32, (8, BLOCK), 1)
    start = jnp.zeros((8, BLOCK), jnp.int32)
    end = jnp.int32(0)
    for j in range(DOCS):
        end = end + length_ref[j]
        start = jnp.where(position >= end, end, start)
    start_ref[...] = start - base


def unpack_small(packed_ref, even_ref, odd_ref):
    even = lax.rem(lax.axis_index("ctx"), 2) == 0
    low, high = (packed_ref[:, h : h + 16, :].reshape(BLOCK, 256) for h in (0, 16))
    even_ref[...] = jnp.where(even, low, high)
    odd_ref[...] = jnp.where(even, high, low)


def dot(a, b, contract):
    return lax.dot_general(a, b, ((contract[:1], contract[1:]), ((), ())), preferred_element_type=F32)


def pair_up(even_ref, odd_ref, before_even, before_odd, even_out, odd_out):
    even_out[0] = even_ref[...]
    even_out[1] = before_even[...]
    odd_out[0] = odd_ref[...]
    odd_out[1] = before_odd[...]


def two_tiles(rows_ref, stat_ref, start_ref, half, first, tiles, put_query):
    key_at = lax.broadcasted_iota(jnp.int32, (BLOCK, BLOCK), 0)
    row_at = lax.broadcasted_iota(jnp.int32, (BLOCK, BLOCK), 1)
    start = start_ref[half : half + 1, :]
    allowed = [key_at - BLOCK * (first + s) >= start for s in range(2)]
    if first == 0:
        allowed[0] = allowed[0] & (key_at <= row_at)
    bias = jnp.concatenate([jnp.where(a, 0.0, MASKED) for a in allowed], axis=0)
    bias = jnp.concatenate([bias, bias], axis=1)
    keys = jnp.concatenate([t[:, :HEAD] for t in tiles], axis=0)
    values = jnp.concatenate([t[:, HEAD:] for t in tiles], axis=0)
    keys_turned = keys.T
    key_total = jnp.zeros((2 * BLOCK, HEAD), F32)
    value_total = jnp.zeros((2 * BLOCK, HEAD), F32)
    rows = slice(half * 16, half * 16 + 16)
    for g in range(0, GROUP, 2):

        def head_pair(offset):
            columns = [slice(offset + n * HEAD, offset + (n + 1) * HEAD) for n in (g, g + 1)]
            return jnp.concatenate([rows_ref[:, rows, c].reshape(BLOCK, HEAD) for c in columns], 0)

        query, grad = head_pair(0), head_pair(1024)
        norm, delta = (
            jnp.concatenate([stat_ref[half, s, n : n + 1, :] for n in (g, g + 1)], axis=1)
            for s in range(2)
        )
        scores = dot(keys, query, (1, 1))
        weights = jnp.exp2(scores * (INV_ROOT * LOG2E) - norm + bias)
        weight_grad = dot(values, grad, (1, 1))
        score_grad = (weights * (weight_grad - delta)).astype(BF)
        value_total += dot(weights.astype(BF), grad, (1, 0))
        key_total += dot(score_grad, query, (1, 0))
        put_query(g, dot(keys_turned, score_grad, (1, 0)))
    return key_total * INV_ROOT, value_total


def near_gradients(
    rows_ref, even_ref, odd_ref, before_even, before_odd, start_ref,
    turned, own_out, near_out, stat_ref, stat_turned,
):
    even = lax.rem(lax.axis_index("ctx"), 2) == 0
    for half in range(2):
        stats = rows_ref[:, half * 16 : half * 16 + 16, 2048:2176].reshape(BLOCK, HEAD)
        stat_turned[...] = stats.astype(F32).T
        stat_ref[half, 0] = (stat_turned[0:8, :] + stat_turned[8:16, :]) * LOG2E
        stat_ref[half, 1] = stat_turned[16:24, :] + stat_turned[24:32, :]
        is_even = even if half == 0 else jnp.logical_not(even)
        tiles = [
            jnp.where(is_even, even_ref[...], odd_ref[...]),
            jnp.where(is_even, before_even[...], before_odd[...]),
        ]

        def put(g, part):
            turned[half, :, g * HEAD : (g + 2) * HEAD] = part

        key_total, value_total = two_tiles(
            rows_ref, stat_ref, start_ref, half, 0, tiles, put
        )
        own_out[half, :, :HEAD] = key_total[:BLOCK]
        own_out[half, :, HEAD:] = value_total[:BLOCK]
        near_out[half, :, :HEAD] = key_total[BLOCK:].astype(BF)
        near_out[half, :, HEAD:] = value_total[BLOCK:].astype(BF)


def far_gradients(
    rows_ref, before_even, before_odd, stat_ref, start_ref, turned, near_ref,
    query_out, send_ref,
):
    ctx = lax.axis_index("ctx")
    member = lax.rem(ctx, 8)
    even = lax.rem(ctx, 2) == 0
    for half in range(2):
        is_even = even if half == 0 else jnp.logical_not(even)
        tiles = [jnp.where(is_even, before_even[s], before_odd[s]) for s in range(2)]

        def put(g, part):
            part = (part + turned[half, :, g * HEAD : (g + 2) * HEAD]) * INV_ROOT
            for n in range(2):
                query_out[half, :, (g + n) * HEAD : (g + n + 1) * HEAD] = (
                    part[:, n * HEAD : (n + 1) * HEAD].T.astype(BF)
                )

        key_total, value_total = two_tiles(
            rows_ref, stat_ref, start_ref, half, 2, tiles, put
        )
        for back in (1, 2, 3):
            slot = lax.rem(member + (back if half else 8 - back), 8)
            if back == 1:
                send_ref[slot] = near_ref[half]
            else:
                part = slice((back - 2) * BLOCK, (back - 1) * BLOCK)
                send_ref[slot, :, :HEAD] = key_total[part].astype(BF)
                send_ref[slot, :, HEAD:] = value_total[part].astype(BF)
    for apart in (0, 4):
        send_ref[lax.rem(member + apart, 8)] = jnp.zeros((BLOCK, 2 * HEAD), BF)


def add_group(own_ref, got_ref, sum_ref, pass_ref):
    member = lax.rem(lax.axis_index("ctx"), 8)
    zero = jnp.zeros((BLOCK, 2 * HEAD), F32)
    low, high, other = own_ref[0], own_ref[1], zero
    for s in range(8):
        got = got_ref[s].astype(F32)
        apart = lax.rem(s - member + 8, 8)
        from_low = (apart >= 1) & (apart <= 3)
        from_high = apart >= 5
        low = low + jnp.where(from_low & (s > member), got, 0.0)
        high = high + jnp.where(from_high & (s < member), got, 0.0)
        other = other + jnp.where((from_low & (s < member)) | (from_high & (s > member)), got, 0.0)
    sum_ref[0] = low
    sum_ref[1] = high
    pass_ref[...] = other.astype(BF)


def add_rest(sum_ref, got_ref, key_out, value_out):
    odd = lax.rem(lax.div(lax.axis_index("ctx"), 4), 2) == 1
    got = got_ref[...].astype(F32)
    for half in range(2):
        pick = odd if half == 0 else jnp.logical_not(odd)
        total = sum_ref[half] + jnp.where(pick, got, 0.0)
        key_out[half] = total[:, :HEAD].astype(BF)
        value_out[half] = total[:, HEAD:].astype(BF)


def between_groups():
    pairs = []
    for x in range(4):
        pairs += [(4 * z + x, 4 * (z + 2) + x) for z in range(0, 13, 2)]
        pairs += [(4 * z + x, 4 * (z - 2) + x) for z in range(3, 16, 2)]
        pairs += [(56 + x, 63 - x)]
    return pairs


def body(lengths, queries, keys, values, outputs, grads, norms):
    last = 2 * lax.axis_size("ctx") - 1

    def owner(p):
        return min(p, last - p)

    def later(first, back):
        return [(owner(p), owner(p + back)) for p in range(first, last + 1 - back, 2)]

    groups = [[8 * m + j for j in range(8)] for m in range(8)]

    def by_head(x):
        return lax.all_to_all(x, "kvh", split_axis=0, concat_axis=0, tiled=True)

    (small,) = call(
        pack_small,
        [((8, 32, 256), BF)],
        2,
        scratch=[pltpu.VMEM((2, 16, 1024), BF)] * 2 + [pltpu.SemaphoreType.DMA((2,))],
        raw=True,
    )(keys, values)
    small = by_head(small)
    large, starts = call(
        pack_large,
        [((8, 32, 2176), BF), ((8, BLOCK), jnp.int32)],
        5,
        smem=(0,),
        scratch=[pltpu.VMEM((2, 16, 8192), BF)] * 3
        + [pltpu.VMEM((2, 16, 64), F32), pltpu.SemaphoreType.DMA((4,))],
        raw=True,
    )(lengths, queries, grads, outputs, norms)
    large = by_head(large)
    tile = ((BLOCK, 256), BF)
    even, odd = call(unpack_small, [tile, tile], 1)(small)
    before_odd = lax.ppermute(even, "ctx", later(0, 1))
    before_even = lax.ppermute(odd, "ctx", later(1, 1))
    pair = ((2, BLOCK, 256), BF)
    even_pair, odd_pair = call(pair_up, [pair, pair], 4)(even, odd, before_even, before_odd)
    even_pair = lax.ppermute(even_pair, "ctx", later(0, 2))
    odd_pair = lax.ppermute(odd_pair, "ctx", later(1, 2))
    turned, own, near, stats = call(
        near_gradients,
        [
            ((2, HEAD, 1024), F32),
            ((2, BLOCK, 256), F32),
            pair,
            ((2, 2, GROUP, BLOCK), F32),
        ],
        6,
        scratch=[pltpu.VMEM((HEAD, BLOCK), F32)],
    )(large, even, odd, before_even, before_odd, starts)
    query_grad, sent = call(
        far_gradients, [((2, BLOCK, 1024), BF), ((8, BLOCK, 256), BF)], 7
    )(large, even_pair, odd_pair, stats, starts, turned, near)
    got = lax.all_to_all(
        sent, "ctx", split_axis=0, concat_axis=0, tiled=True, axis_index_groups=groups
    )
    sums, passed = call(add_group, [((2, BLOCK, 256), F32), tile], 2)(own, got)
    passed = lax.ppermute(passed, "ctx", between_groups())
    key_grad, value_grad = call(add_rest, [((2, BLOCK, HEAD), BF)] * 2, 2)(sums, passed)
    return query_grad, key_grad, value_grad


def solution(mesh):
    rows = P(None, ("ctx", "kvh"), None)
    heads = P(None, "ctx", "kvh")
    return jax.shard_map(
        body,
        mesh=mesh,
        in_specs=(P(),) + (rows,) * 6,
        out_specs=(heads,) * 3,
        check_vma=False,
    )
```

time: 82.9 us -> 70.8 us (0.85)
  the two profiles are of different devices: /device:TPU:424 before, /device:TPU:8 now
where the time goes in v2:
time: 70.8 us; the launch traced here: 70.3 us
  starting transfers between devices  32.8 us (46%)
  blocking collectives  14.1 us (20%)
  waiting for transfers between devices  11.5 us (16%)
  Pallas kernels  11.2 us (16%)
  between operations  0.72 us (1%)
    all_to_all x2, starting transfers between devices, by_head(): return lax.all_to_all(x, 'kvh', split_axis=0, concat_axis=0, tiled=True)  14.2 us
    all_to_all x1, blocking collectives, body(): lax.all_to_all(sent, 'ctx', split_axis=0, concat_axis=0, tiled=True, axis...  14.1 us
    ppermute x1, starting transfers between devices, body(): passed = lax.ppermute(passed, 'ctx', between_groups())  8.81 us
    ppermute x1, starting transfers between devices, body(): even_pair = lax.ppermute(even_pair, 'ctx', later(0, 2))  5.9 us
    pallas_call x1, Pallas kernels, body(): call(pack_large, [((8, 32, 2176), BF), ((8, BLOCK), jnp.int32)], 5, smem=...  3.67 us
    ppermute x1, waiting for transfers between devices, body(): before_odd = lax.ppermute(even, 'ctx', later(0, 1))  3.56 us
    ppermute x1, waiting for transfers between devices, body(): odd_pair = lax.ppermute(odd_pair, 'ctx', later(1, 2))  3.17 us
    pallas_call x1, Pallas kernels, body(): call(far_gradients, [((2, BLOCK, 1024), BF), ((8, BLOCK, 256), BF)], 7)  2.9 us
  transfers between devices with their start and end apart: 7, of which 5 were waited for; matrix products, arithmetic and copies ran while one was open for 0% of the time, Pallas kernels for 8%

profile of v2, /device:TPU:8, one launch (start us, length us, event | category | flops | bytes accessed | tf_op | source)
XLA Modules:
  0.0 70.3 jit_solution(17890229601916499708)
XLA Ops:
  0.6 1.6 %shard_map.95 = bf16[8,32,256]{2,1,0:T(8,128)(2,1)} custom-call(bf16[2,16,1024]{2,1,0:T(8,128)(2,1)} %key_raw.1, bf16[2,16,1024]{2,1,0:T(8,128)(2,1)} %value_raw.1), custom_call_target="tpu_custom_call" | custom-call | tf_op jit(solution)/shard_map/pallas_call | solution.py:262
  2.2 9.1 %all-to-all-start.1 = ((bf16[8,32,256]{2,1,0:T(8,128)(2,1)}), bf16[8,32,256]{2,1,0:T(8,128)(2,1)S(1)}, u32[]{:S(2)}, u32[]{:S(2)}) async-start(bf16[8,32,256]{2,1,0:T(8,128)(2,1)} %shard_map.95), calls=%async_computation.1 | async-start | bytes 262144 | tf_op jit(solution)/shard_map/all_to_all | solution.py:260
  11.3 3.7 %shard_map.94 = (bf16[8,32,2176]{2,1,0:T(8,128)(2,1)}, s32[8,128]{1,0:T(8,128)}) custom-call(s32[64]{0:T(128)} %length_ref.1, bf16[2,16,8192]{2,1,0:T(8,128)(2,1)} %refs_0_.1, bf16[2,16,8192]{2,1,0:T(8,128)(2,1)} %refs_1_.1, bf16[2,16,8192]{2,1,0:T(8,128)(2,1)} %refs_2_.1, f32[2,16,64]{2,1,0:T(8,128)} %refs_3_.1), custom_call_target="tpu_custom_call" | custom-call | tf_op jit(solution)/shard_map/pallas_call | solution.py:270
  15.0 1.0 %all-to-all-done.1.packed_ref = bf16[8,32,256]{2,1,0:T(8,128)(2,1)S(1)} async-done(((bf16[8,32,256]{2,1,0:T(8,128)(2,1)}), bf16[8,32,256]{2,1,0:T(8,128)(2,1)S(1)}, u32[]{:S(2)}, u32[]{:S(2)}) %all-to-all-start.1) | async-done | bytes 131104 | tf_op jit(solution)/shard_map/all_to_all | solution.py:260
  16.0 0.0 copy-start
  16.0 5.0 %all-to-all-start = ((bf16[8,32,2176]{2,1,0:T(8,128)(2,1)}), bf16[8,32,2176]{2,1,0:T(8,128)(2,1)S(1)}, u32[]{:S(2)}, u32[]{:S(2)}) async-start(bf16[8,32,2176]{2,1,0:T(8,128)(2,1)} %get-tuple-element.19), calls=%async_computation | async-start | bytes 2228224 | tf_op jit(solution)/shard_map/all_to_all | solution.py:260
  21.1 1.9 %collective-permute-start.1 = (bf16[128,256]{1,0:T(8,128)(2,1)S(1)}, bf16[128,256]{1,0:T(8,128)(2,1)S(1)}, u32[]{:S(2)}, u32[]{:S(2)}) collective-permute-start(bf16[128,256]{1,0:T(8,128)(2,1)S(1)} %get-tuple-element.20.even_ref), channel_id=1, source_target_pairs={{0,8},{16,24},{32,40},{48,56},{64,72},{80,88},{96,104},{112,120},{... | collective-permute-start | bytes 196616 | tf_op jit(solution)/shard_map/ppermute | solution.py:282
  23.0 0.7 collective-permute-start
  23.7 3.6 %collective-permute-done.1.before_odd = bf16[128,256]{1,0:T(8,128)(2,1)S(1)} collective-permute-done((bf16[128,256]{1,0:T(8,128)(2,1)S(1)}, bf16[128,256]{1,0:T(8,128)(2,1)S(1)}, u32[]{:S(2)}, u32[]{:S(2)}) %collective-permute-start.1) | collective-permute-done | bytes 65568 | tf_op jit(solution)/shard_map/ppermute | solution.py:282
  27.3 0.0 collective-permute-done.before_even
  27.3 5.9 %collective-permute-start.2 = (bf16[2,128,256]{2,1,0:T(8,128)(2,1)S(1)}, bf16[2,128,256]{2,1,0:T(8,128)(2,1)S(1)}, u32[]{:S(2)}, u32[]{:S(2)}) collective-permute-start(bf16[2,128,256]{2,1,0:T(8,128)(2,1)S(1)} %get-tuple-element.22), channel_id=1, source_target_pairs={{0,16},{16,32},{32,48},{48,64},{64,80},{80,96},{96,112},{112,128},... | collective-permute-start | bytes 393224 | tf_op jit(solution)/shard_map/ppermute | solution.py:286
  33.2 1.3 %collective-permute-start.3 = (bf16[2,128,256]{2,1,0:T(8,128)(2,1)S(1)}, bf16[2,128,256]{2,1,0:T(8,128)(2,1)S(1)}, u32[]{:S(2)}, u32[]{:S(2)}) collective-permute-start(bf16[2,128,256]{2,1,0:T(8,128)(2,1)S(1)} %get-tuple-element.23), channel_id=1, source_target_pairs={{8,24},{24,40},{40,56},{56,72},{72,88},{88,104},{104,120},{120,136... | collective-permute-start | bytes 393224 | tf_op jit(solution)/shard_map/ppermute | solution.py:287
  34.5 1.8 %all-to-all-done.rows_ref = bf16[8,32,2176]{2,1,0:T(8,128)(2,1)S(1)} async-done(((bf16[8,32,2176]{2,1,0:T(8,128)(2,1)}), bf16[8,32,2176]{2,1,0:T(8,128)(2,1)S(1)}, u32[]{:S(2)}, u32[]{:S(2)}) %all-to-all-start) | async-done | bytes 1114144 | tf_op jit(solution)/shard_map/all_to_all | solution.py:260
  36.3 0.0 copy-done
  36.3 2.1 %shard_map.98 = (f32[2,128,1024]{2,1,0:T(8,128)S(1)}, f32[2,128,256]{2,1,0:T(8,128)S(1)}, bf16[2,128,256]{2,1,0:T(8,128)(2,1)S(1)}, f32[2,2,8,128]{3,2,1,0:T(8,128)S(1)}) custom-call(bf16[8,32,2176]{2,1,0:T(8,128)(2,1)S(1)} %all-to-all-done.rows_ref, bf16[128,256]{1,0:T(8,128)(2,1)S(1)} %get-tuple-element.20.even_ref, ...), custom_call_target="tpu_custom_call" | custom-call | tf_op jit(solution)/shard_map/pallas_call | solution.py:288
  38.4 0.0 collective-permute-done.2.before_even
  38.4 3.2 %collective-permute-done.3.before_odd = bf16[2,128,256]{2,1,0:T(8,128)(2,1)S(1)} collective-permute-done((bf16[2,128,256]{2,1,0:T(8,128)(2,1)S(1)}, bf16[2,128,256]{2,1,0:T(8,128)(2,1)S(1)}, u32[]{:S(2)}, u32[]{:S(2)}) %collective-permute-start.3) | collective-permute-done | bytes 131104 | tf_op jit(solution)/shard_map/ppermute | solution.py:287
  41.6 2.9 %shard_map.99 = (bf16[2,128,1024]{2,1,0:T(8,128)(2,1)}, bf16[8,128,256]{2,1,0:T(8,128)(2,1)S(1)}) custom-call(bf16[8,32,2176]{2,1,0:T(8,128)(2,1)S(1)} %all-to-all-done.rows_ref, bf16[2,128,256]{2,1,0:T(8,128)(2,1)S(1)} %collective-permute-done.2.before_even, bf16[2,128,256]{2,1,0:T(8,128)(2,1)S(1)} %collective-permute-done.3.before_odd, ...), custom_call_target="tpu_custom_call" | custom-call | tf_op jit(solution)/shard_map/pallas_call | solution.py:299
  44.5 14.1 %all_to_all.15.got_ref = bf16[8,128,256]{2,1,0:T(8,128)(2,1)S(1)} all-to-all(bf16[8,128,256]{2,1,0:T(8,128)(2,1)S(1)} %get-tuple-element.30), channel_id=1, replica_groups={{0,8,16,24,32,40,48,56},{64,72,80,88,96,104,112,120},{128,136,144,152,1..., dimensions={0} | all-to-all | bytes 1048576 | tf_op jit(solution)/shard_map/all_to_all | solution.py:302
  58.6 0.3 shard_map.100
  58.9 8.8 %collective-permute-start.4 = (bf16[128,256]{1,0:T(8,128)(2,1)S(1)}, bf16[128,256]{1,0:T(8,128)(2,1)S(1)}, u32[]{:S(2)}, u32[]{:S(2)}) collective-permute-start(bf16[128,256]{1,0:T(8,128)(2,1)S(1)} %get-tuple-element.32), channel_id=1, source_target_pairs={{0,64},{64,128},{128,192},{192,256},{256,320},{320,384},{384,448},... | collective-permute-start | bytes 196616 | tf_op jit(solution)/shard_map/ppermute | solution.py:306
  67.7 1.9 %collective-permute-done.4.got_ref = bf16[128,256]{1,0:T(8,128)(2,1)S(1)} collective-permute-done((bf16[128,256]{1,0:T(8,128)(2,1)S(1)}, bf16[128,256]{1,0:T(8,128)(2,1)S(1)}, u32[]{:S(2)}, u32[]{:S(2)}) %collective-permute-start.4) | collective-permute-done | bytes 65568 | tf_op jit(solution)/shard_map/ppermute | solution.py:306
  69.6 0.7 shard_map.101
  (2 shorter events, 0.0 us)
Async XLA Ops:
  2.2 13.8 %all-to-all-start.1 = ((bf16[8,32,256]{2,1,0:T(8,128)(2,1)}), bf16[8,32,256]{2,1,0:T(8,128)(2,1)S(1)}, u32[]{:S(2)}, u32[]{:S(2)}) async-start(bf16[8,32,256]{2,1,0:T(8,128)(2,1)} %shard_map.95), calls=%async_computation.1 | async-start | bytes 262144 | tf_op jit(solution)/shard_map/all_to_all | solution.py:260
  16.0 20.3 %copy-start = (s32[8,128]{1,0:T(8,128)S(1)}, s32[8,128]{1,0:T(8,128)}, u32[]{:S(2)}) copy-start(s32[8,128]{1,0:T(8,128)} %get-tuple-element.24.start_ref) | copy-start | bytes 12292
  16.0 20.3 %all-to-all-start = ((bf16[8,32,2176]{2,1,0:T(8,128)(2,1)}), bf16[8,32,2176]{2,1,0:T(8,128)(2,1)S(1)}, u32[]{:S(2)}, u32[]{:S(2)}) async-start(bf16[8,32,2176]{2,1,0:T(8,128)(2,1)} %get-tuple-element.19), calls=%async_computation | async-start | bytes 2228224 | tf_op jit(solution)/shard_map/all_to_all | solution.py:260
  21.1 6.2 %collective-permute-start.1 = (bf16[128,256]{1,0:T(8,128)(2,1)S(1)}, bf16[128,256]{1,0:T(8,128)(2,1)S(1)}, u32[]{:S(2)}, u32[]{:S(2)}) collective-permute-start(bf16[128,256]{1,0:T(8,128)(2,1)S(1)} %get-tuple-element.20.even_ref), channel_id=1, source_target_pairs={{0,8},{16,24},{32,40},{48,56},{64,72},{80,88},{96,104},{112,120},{... | collective-permute-start | bytes 196616 | tf_op jit(solution)/shard_map/ppermute | solution.py:282
  23.0 4.2 %collective-permute-start = (bf16[128,256]{1,0:T(8,128)(2,1)S(1)}, bf16[128,256]{1,0:T(8,128)(2,1)S(1)}, u32[]{:S(2)}, u32[]{:S(2)}) collective-permute-start(bf16[128,256]{1,0:T(8,128)(2,1)S(1)} %get-tuple-element.21.odd_ref), channel_id=1, source_target_pairs={{8,16},{24,32},{40,48},{56,64},{72,80},{88,96},{104,112},{120,128}... | collective-permute-start | bytes 196616 | tf_op jit(solution)/shard_map/ppermute | solution.py:283
  27.3 11.1 %collective-permute-start.2 = (bf16[2,128,256]{2,1,0:T(8,128)(2,1)S(1)}, bf16[2,128,256]{2,1,0:T(8,128)(2,1)S(1)}, u32[]{:S(2)}, u32[]{:S(2)}) collective-permute-start(bf16[2,128,256]{2,1,0:T(8,128)(2,1)S(1)} %get-tuple-element.22), channel_id=1, source_target_pairs={{0,16},{16,32},{32,48},{48,64},{64,80},{80,96},{96,112},{112,128},... | collective-permute-start | bytes 393224 | tf_op jit(solution)/shard_map/ppermute | solution.py:286
  33.2 8.4 %collective-permute-start.3 = (bf16[2,128,256]{2,1,0:T(8,128)(2,1)S(1)}, bf16[2,128,256]{2,1,0:T(8,128)(2,1)S(1)}, u32[]{:S(2)}, u32[]{:S(2)}) collective-permute-start(bf16[2,128,256]{2,1,0:T(8,128)(2,1)S(1)} %get-tuple-element.23), channel_id=1, source_target_pairs={{8,24},{24,40},{40,56},{56,72},{72,88},{88,104},{104,120},{120,136... | collective-permute-start | bytes 393224 | tf_op jit(solution)/shard_map/ppermute | solution.py:287
  58.9 10.7 %collective-permute-start.4 = (bf16[128,256]{1,0:T(8,128)(2,1)S(1)}, bf16[128,256]{1,0:T(8,128)(2,1)S(1)}, u32[]{:S(2)}, u32[]{:S(2)}) collective-permute-start(bf16[128,256]{1,0:T(8,128)(2,1)S(1)} %get-tuple-element.32), channel_id=1, source_target_pairs={{0,64},{64,128},{128,192},{192,256},{256,320},{320,384},{384,448},... | collective-permute-start | bytes 196616 | tf_op jit(solution)/shard_map/ppermute | solution.py:306

commit v3 on v2

--- a/solution.py
+++ b/solution.py
@@ -94,39 +94,49 @@
     start_ref[...] = start - base
 
 
-def unpack_small(packed_ref, even_ref, odd_ref):
-    even = lax.rem(lax.axis_index("ctx"), 2) == 0
+def unpack_small(packed_ref, own_ref, third_ref):
+    odd = lax.rem(lax.axis_index("ctx"), 2) == 1
     low, high = (packed_ref[:, h : h + 16, :].reshape(BLOCK, 256) for h in (0, 16))
-    even_ref[...] = jnp.where(even, low, high)
-    odd_ref[...] = jnp.where(even, high, low)
+    own_ref[0] = low
+    own_ref[1] = high
+    third_ref[...] = jnp.where(odd, low, high)
 
 
 def dot(a, b, contract):
     return lax.dot_general(a, b, ((contract[:1], contract[1:]), ((), ())), preferred_element_type=F32)
 
 
-def pair_up(even_ref, odd_ref, before_even, before_odd, even_out, odd_out):
-    even_out[0] = even_ref[...]
-    even_out[1] = before_even[...]
-    odd_out[0] = odd_ref[...]
-    odd_out[1] = before_odd[...]
-
-
-def two_tiles(rows_ref, stat_ref, start_ref, half, first, tiles, put_query):
+def pair_up(own_ref, mate_ref, first_out, second_out):
+    ctx = lax.axis_index("ctx")
+    odd = lax.rem(ctx, 2) == 1
+    swapped = lax.rem(lax.div(ctx, 2), 2) == 1
+    low, high = ((own_ref[h], mate_ref[h]) for h in range(2))
+    low = [jnp.where(odd, low[s], low[1 - s]) for s in range(2)]
+    high = [jnp.where(odd, high[1 - s], high[s]) for s in range(2)]
+    for s in range(2):
+        first_out[s] = jnp.where(swapped, high[s], low[s])
+        second_out[s] = jnp.where(swapped, low[s], high[s])
+
+
+def rows_of(half):
+    return pl.ds(pl.multiple_of(half * 16, 16), 16)
+
+
+def tile_gradients(rows_ref, stat_ref, start_ref, half, backs, tiles, put_query):
     key_at = lax.broadcasted_iota(jnp.int32, (BLOCK, BLOCK), 0)
     row_at = lax.broadcasted_iota(jnp.int32, (BLOCK, BLOCK), 1)
-    start = start_ref[half : half + 1, :]
-    allowed = [key_at - BLOCK * (first + s) >= start for s in range(2)]
-    if first == 0:
+    start = start_ref[pl.ds(half, 1), :]
+    allowed = [key_at - BLOCK * back >= start for back in backs]
+    if backs[0] == 0:
         allowed[0] = allowed[0] & (key_at <= row_at)
     bias = jnp.concatenate([jnp.where(a, 0.0, MASKED) for a in allowed], axis=0)
     bias = jnp.concatenate([bias, bias], axis=1)
     keys = jnp.concatenate([t[:, :HEAD] for t in tiles], axis=0)
     values = jnp.concatenate([t[:, HEAD:] for t in tiles], axis=0)
     keys_turned = keys.T
-    key_total = jnp.zeros((2 * BLOCK, HEAD), F32)
-    value_total = jnp.zeros((2 * BLOCK, HEAD), F32)
-    rows = slice(half * 16, half * 16 + 16)
+    key_total = jnp.zeros(keys.shape, F32)
+    value_total = jnp.zeros(keys.shape, F32)
+    rows = rows_of(half)
     for g in range(0, GROUP, 2):
 
         def head_pair(offset):
@@ -148,44 +158,49 @@
     return key_total * INV_ROOT, value_total
 
 
+def halves():
+    even = 1 - lax.rem(lax.axis_index("ctx"), 2)
+    return even, 1 - even
+
+
 def near_gradients(
-    rows_ref, even_ref, odd_ref, before_even, before_odd, start_ref,
-    turned, own_out, near_out, stat_ref, stat_turned,
+    rows_ref, own_ref, mate_ref, start_ref, turned, own_out, near_out, stat_ref, stat_turned
 ):
-    even = lax.rem(lax.axis_index("ctx"), 2) == 0
-    for half in range(2):
-        stats = rows_ref[:, half * 16 : half * 16 + 16, 2048:2176].reshape(BLOCK, HEAD)
+    for mated, half in zip((True, False), halves()):
+        stats = rows_ref[:, rows_of(half), 2048:2176].reshape(BLOCK, HEAD)
         stat_turned[...] = stats.astype(F32).T
         stat_ref[half, 0] = (stat_turned[0:8, :] + stat_turned[8:16, :]) * LOG2E
         stat_ref[half, 1] = stat_turned[16:24, :] + stat_turned[24:32, :]
-        is_even = even if half == 0 else jnp.logical_not(even)
-        tiles = [
-            jnp.where(is_even, even_ref[...], odd_ref[...]),
-            jnp.where(is_even, before_even[...], before_odd[...]),
-        ]
 
         def put(g, part):
             turned[half, :, g * HEAD : (g + 2) * HEAD] = part
 
-        key_total, value_total = two_tiles(
-            rows_ref, stat_ref, start_ref, half, 0, tiles, put
+        tiles, backs = [own_ref[half]], (0,)
+        if mated:
+            tiles, backs = tiles + [mate_ref[half]], (0, 1)
+        key_total, value_total = tile_gradients(
+            rows_ref, stat_ref, start_ref, half, backs, tiles, put
         )
         own_out[half, :, :HEAD] = key_total[:BLOCK]
         own_out[half, :, HEAD:] = value_total[:BLOCK]
-        near_out[half, :, :HEAD] = key_total[BLOCK:].astype(BF)
-        near_out[half, :, HEAD:] = value_total[BLOCK:].astype(BF)
+        if mated:
+            near_out[:, :HEAD] = key_total[BLOCK:].astype(BF)
+            near_out[:, HEAD:] = value_total[BLOCK:].astype(BF)
 
 
 def far_gradients(
-    rows_ref, before_even, before_odd, stat_ref, start_ref, turned, near_ref,
+    rows_ref, first_ref, second_ref, third_ref, stat_ref, start_ref, turned, near_ref,
     query_out, send_ref,
 ):
     ctx = lax.axis_index("ctx")
     member = lax.rem(ctx, 8)
-    even = lax.rem(ctx, 2) == 0
-    for half in range(2):
-        is_even = even if half == 0 else jnp.logical_not(even)
-        tiles = [jnp.where(is_even, before_even[s], before_odd[s]) for s in range(2)]
+    swapped = lax.rem(lax.div(ctx, 2), 2) == 1
+    for mated, half in zip((True, False), halves()):
+        from_first = swapped == (half == 0)
+        tiles = [jnp.where(from_first, first_ref[s], second_ref[s]) for s in range(2)]
+        backs = (2, 3)
+        if not mated:
+            tiles, backs = tiles + [third_ref[...]], (1, 2, 3)
 
         def put(g, part):
             part = (part + turned[half, :, g * HEAD : (g + 2) * HEAD]) * INV_ROOT
@@ -194,17 +209,19 @@
                     part[:, n * HEAD : (n + 1) * HEAD].T.astype(BF)
                 )
 
-        key_total, value_total = two_tiles(
-            rows_ref, stat_ref, start_ref, half, 2, tiles, put
+        key_total, value_total = tile_gradients(
+            rows_ref, stat_ref, start_ref, half, backs, tiles, put
         )
-        for back in (1, 2, 3):
-            slot = lax.rem(member + (back if half else 8 - back), 8)
-            if back == 1:
-                send_ref[slot] = near_ref[half]
-            else:
-                part = slice((back - 2) * BLOCK, (back - 1) * BLOCK)
-                send_ref[slot, :, :HEAD] = key_total[part].astype(BF)
-                send_ref[slot, :, HEAD:] = value_total[part].astype(BF)
+
+        def slot(back):
+            return lax.rem(member + jnp.where(half == 1, back, 8 - back), 8)
+
+        if mated:
+            send_ref[slot(1)] = near_ref[...]
+        for s, back in enumerate(backs):
+            part = slice(s * BLOCK, (s + 1) * BLOCK)
+            send_ref[slot(back), :, :HEAD] = key_total[part].astype(BF)
+            send_ref[slot(back), :, HEAD:] = value_total[part].astype(BF)
     for apart in (0, 4):
         send_ref[lax.rem(member + apart, 8)] = jnp.zeros((BLOCK, 2 * HEAD), BF)
 
@@ -246,14 +263,13 @@
 
 
 def body(lengths, queries, keys, values, outputs, grads, norms):
-    last = 2 * lax.axis_size("ctx") - 1
-
-    def owner(p):
-        return min(p, last - p)
-
-    def later(first, back):
-        return [(owner(p), owner(p + back)) for p in range(first, last + 1 - back, 2)]
-
+    count = lax.axis_size("ctx")
+    mates = [(i, i ^ 1) for i in range(count)]
+    first_step = [(i, i ^ 2) for i in range(count)]
+    second_step = [(i, i + 2 if i % 4 >= 2 else i - 2) for i in range(2, count - 2)]
+    second_step += [(i, i) for i in (count - 2, count - 1)]
+    third_step = [(i, i + 3) for i in range(1, count - 3, 2)]
+    third_step += [(j, i) for i, j in third_step] + [(count - 3, count - 1), (count - 1, count - 3)]
     groups = [[8 * m + j for j in range(8)] for m in range(8)]
 
     def by_head(x):
@@ -278,27 +294,27 @@
     )(lengths, queries, grads, outputs, norms)
     large = by_head(large)
     tile = ((BLOCK, 256), BF)
-    even, odd = call(unpack_small, [tile, tile], 1)(small)
-    before_odd = lax.ppermute(even, "ctx", later(0, 1))
-    before_even = lax.ppermute(odd, "ctx", later(1, 1))
     pair = ((2, BLOCK, 256), BF)
-    even_pair, odd_pair = call(pair_up, [pair, pair], 4)(even, odd, before_even, before_odd)
-    even_pair = lax.ppermute(even_pair, "ctx", later(0, 2))
-    odd_pair = lax.ppermute(odd_pair, "ctx", later(1, 2))
+    held, third = call(unpack_small, [pair, tile], 1)(small)
+    mate = lax.ppermute(held, "ctx", mates)
+    third = lax.ppermute(third, "ctx", third_step)
+    first, second = call(pair_up, [pair, pair], 2)(held, mate)
+    first = lax.ppermute(first, "ctx", first_step)
+    second = lax.ppermute(second, "ctx", second_step)
     turned, own, near, stats = call(
         near_gradients,
         [
             ((2, HEAD, 1024), F32),
             ((2, BLOCK, 256), F32),
-            pair,
+            tile,
             ((2, 2, GROUP, BLOCK), F32),
         ],
-        6,
+        4,
         scratch=[pltpu.VMEM((HEAD, BLOCK), F32)],
-    )(large, even, odd, before_even, before_odd, starts)
+    )(large, held, mate, starts)
     query_grad, sent = call(
-        far_gradients, [((2, BLOCK, 1024), BF), ((8, BLOCK, 256), BF)], 7
-    )(large, even_pair, odd_pair, stats, starts, turned, near)
+        far_gradients, [((2, BLOCK, 1024), BF), ((8, BLOCK, 256), BF)], 8
+    )(large, first, second, third, stats, starts, turned, near)
     got = lax.all_to_all(
         sent, "ctx", split_axis=0, concat_axis=0, tiled=True, axis_index_groups=groups
     )

time: 70.8 us -> 68.1 us (0.962)
  starting transfers between devices: 32.8 us -> 26.7 us
  blocking collectives: 14.1 us -> 16 us
  waiting for transfers between devices: 11.5 us -> 12.9 us
    ppermute x4, starting transfers between devices: 9.78 us -> 5.17 us  [the longest x1 1.92 us: body(): mate = lax.ppermute(held, 'ctx', mates)]
    all_to_all x2, waiting for transfers between devices: 2.84 us -> 5.48 us  [by_head(): return lax.all_to_all(x, 'kvh', split_axis=0, concat_axis=0, tiled=True)]
    all_to_all x1, blocking collectives: 14.1 us -> 16 us  [body(): lax.all_to_all(sent, 'ctx', split_axis=0, concat_axis=0, tiled=True, axis...]
    ppermute x1, starting transfers between devices: 8.81 us -> 7.35 us  [body(): passed = lax.ppermute(passed, 'ctx', between_groups())]
    ppermute x4, waiting for transfers between devices: 6.73 us -> 5.52 us  [the longest x1 5.52 us: body(): mate = lax.ppermute(held, 'ctx', mates)]
  transfers between devices with their start and end apart: 7 -> 7, of which waited for: 5 -> 4; matrix products, arithmetic and copies ran while one was open for 0% -> 0% of each run, Pallas kernels for 8% -> 8%
where the time goes in v3:
time: 68.1 us; the launch traced here: 67.6 us
  starting transfers between devices  26.7 us (39%)
  blocking collectives  16 us (23%)
  waiting for transfers between devices  12.9 us (19%)
  Pallas kernels  11.3 us (17%)
  between operations  0.74 us (1%)
    all_to_all x1, blocking collectives, body(): lax.all_to_all(sent, 'ctx', split_axis=0, concat_axis=0, tiled=True, axis...  16 us
    all_to_all x2, starting transfers between devices, by_head(): return lax.all_to_all(x, 'kvh', split_axis=0, concat_axis=0, tiled=True)  14.2 us
    ppermute x1, starting transfers between devices, body(): passed = lax.ppermute(passed, 'ctx', between_groups())  7.35 us
    ppermute x1, waiting for transfers between devices, body(): mate = lax.ppermute(held, 'ctx', mates)  5.52 us
    all_to_all x2, waiting for transfers between devices, by_head(): return lax.all_to_all(x, 'kvh', split_axis=0, concat_axis=0, tiled=True)  5.48 us
    pallas_call x1, Pallas kernels, body(): call(pack_large, [((8, 32, 2176), BF), ((8, BLOCK), jnp.int32)], 5, smem=...  3.67 us
    pallas_call x1, Pallas kernels, body(): call(far_gradients, [((2, BLOCK, 1024), BF), ((8, BLOCK, 256), BF)], 8)  3.19 us
    ppermute x1, starting transfers between devices, body(): mate = lax.ppermute(held, 'ctx', mates)  1.92 us
  transfers between devices with their start and end apart: 7, of which 4 were waited for; matrix products, arithmetic and copies ran while one was open for 0% of the time, Pallas kernels for 8%

profile of v3, /device:TPU:8, one launch (start us, length us, event | category | flops | bytes accessed | tf_op | source)
XLA Modules:
  0.0 67.6 jit_solution(3138889296418958105)
XLA Ops:
  0.6 1.6 %shard_map.95 = bf16[8,32,256]{2,1,0:T(8,128)(2,1)} custom-call(bf16[2,16,1024]{2,1,0:T(8,128)(2,1)} %key_raw.1, bf16[2,16,1024]{2,1,0:T(8,128)(2,1)} %value_raw.1), custom_call_target="tpu_custom_call" | custom-call | tf_op jit(solution)/shard_map/pallas_call | solution.py:278
  2.2 9.1 %all-to-all-start.1 = ((bf16[8,32,256]{2,1,0:T(8,128)(2,1)}), bf16[8,32,256]{2,1,0:T(8,128)(2,1)S(1)}, u32[]{:S(2)}, u32[]{:S(2)}) async-start(bf16[8,32,256]{2,1,0:T(8,128)(2,1)} %shard_map.95), calls=%async_computation.1 | async-start | bytes 262144 | tf_op jit(solution)/shard_map/all_to_all | solution.py:276
  11.3 3.7 %shard_map.94 = (bf16[8,32,2176]{2,1,0:T(8,128)(2,1)}, s32[8,128]{1,0:T(8,128)}) custom-call(s32[64]{0:T(128)} %length_ref.1, bf16[2,16,8192]{2,1,0:T(8,128)(2,1)} %refs_0_.1, bf16[2,16,8192]{2,1,0:T(8,128)(2,1)} %refs_1_.1, bf16[2,16,8192]{2,1,0:T(8,128)(2,1)} %refs_2_.1, f32[2,16,64]{2,1,0:T(8,128)} %refs_3_.1), custom_call_target="tpu_custom_call" | custom-call | tf_op jit(solution)/shard_map/pallas_call | solution.py:286
  15.0 1.0 %all-to-all-done.1.packed_ref = bf16[8,32,256]{2,1,0:T(8,128)(2,1)S(1)} async-done(((bf16[8,32,256]{2,1,0:T(8,128)(2,1)}), bf16[8,32,256]{2,1,0:T(8,128)(2,1)S(1)}, u32[]{:S(2)}, u32[]{:S(2)}) %all-to-all-start.1) | async-done | bytes 131104 | tf_op jit(solution)/shard_map/all_to_all | solution.py:276
  16.0 0.0 copy-start
  16.0 5.0 %all-to-all-start = ((bf16[8,32,2176]{2,1,0:T(8,128)(2,1)}), bf16[8,32,2176]{2,1,0:T(8,128)(2,1)S(1)}, u32[]{:S(2)}, u32[]{:S(2)}) async-start(bf16[8,32,2176]{2,1,0:T(8,128)(2,1)} %get-tuple-element.19), calls=%async_computation | async-start | bytes 2228224 | tf_op jit(solution)/shard_map/all_to_all | solution.py:276
  21.1 1.9 %collective-permute-start = (bf16[2,128,256]{2,1,0:T(8,128)(2,1)S(1)}, bf16[2,128,256]{2,1,0:T(8,128)(2,1)S(1)}, u32[]{:S(2)}, u32[]{:S(2)}) collective-permute-start(bf16[2,128,256]{2,1,0:T(8,128)(2,1)S(1)} %get-tuple-element.20.own_ref), channel_id=1, source_target_pairs={{0,8},{8,0},{16,24},{24,16},{32,40},{40,32},{48,56},{56,48},{64,72... | collective-permute-start | bytes 393224 | tf_op jit(solution)/shard_map/ppermute | solution.py:299
  23.0 5.5 %collective-permute-done.mate_ref = bf16[2,128,256]{2,1,0:T(8,128)(2,1)S(1)} collective-permute-done((bf16[2,128,256]{2,1,0:T(8,128)(2,1)S(1)}, bf16[2,128,256]{2,1,0:T(8,128)(2,1)S(1)}, u32[]{:S(2)}, u32[]{:S(2)}) %collective-permute-start) | collective-permute-done | bytes 131104 | tf_op jit(solution)/shard_map/ppermute | solution.py:299
  28.6 1.9 %collective-permute-start.1 = (bf16[2,128,256]{2,1,0:T(8,128)(2,1)S(1)}, bf16[2,128,256]{2,1,0:T(8,128)(2,1)S(1)}, u32[]{:S(2)}, u32[]{:S(2)}) collective-permute-start(bf16[2,128,256]{2,1,0:T(8,128)(2,1)S(1)} %get-tuple-element.21), channel_id=1, source_target_pairs={{0,16},{8,24},{16,0},{24,8},{32,48},{40,56},{48,32},{56,40},{64,80... | collective-permute-start | bytes 393224 | tf_op jit(solution)/shard_map/ppermute | solution.py:302
  30.5 0.7 collective-permute-start.2
  31.2 0.7 collective-permute-start.3
  31.9 4.4 %all-to-all-done.rows_ref = bf16[8,32,2176]{2,1,0:T(8,128)(2,1)S(1)} async-done(((bf16[8,32,2176]{2,1,0:T(8,128)(2,1)}), bf16[8,32,2176]{2,1,0:T(8,128)(2,1)S(1)}, u32[]{:S(2)}, u32[]{:S(2)}) %all-to-all-start) | async-done | bytes 1114144 | tf_op jit(solution)/shard_map/all_to_all | solution.py:276
  36.3 0.0 copy-done
  36.3 1.9 %shard_map.98 = (f32[2,128,1024]{2,1,0:T(8,128)S(1)}, f32[2,128,256]{2,1,0:T(8,128)S(1)}, bf16[128,256]{1,0:T(8,128)(2,1)S(1)}, f32[2,2,8,128]{3,2,1,0:T(8,128)S(1)}) custom-call(bf16[8,32,2176]{2,1,0:T(8,128)(2,1)S(1)} %all-to-all-done.rows_ref, bf16[2,128,256]{2,1,0:T(8,128)(2,1)S(1)} %get-tuple-element.20.own_ref, ...), custom_call_target="tpu_custom_call" | custom-call | tf_op jit(solution)/shard_map/pallas_call | solution.py:304
  38.2 0.0 collective-permute-done.3.third_ref
  38.2 0.0 collective-permute-done.1.first_ref
  38.2 0.0 collective-permute-done.2.second_ref
  38.3 3.2 %shard_map.99 = (bf16[2,128,1024]{2,1,0:T(8,128)(2,1)}, bf16[8,128,256]{2,1,0:T(8,128)(2,1)S(1)}) custom-call(bf16[8,32,2176]{2,1,0:T(8,128)(2,1)S(1)} %all-to-all-done.rows_ref, bf16[2,128,256]{2,1,0:T(8,128)(2,1)S(1)} %collective-permute-done.1.first_ref, bf16[2,128,256]{2,1,0:T(8,128)(2,1)S(1)} %collective-permute-done.2.second_ref, ...), custom_call_target="tpu_custom_call" | custom-call | tf_op jit(solution)/shard_map/pallas_call | solution.py:315
  41.4 16.0 %all_to_all.15.got_ref = bf16[8,128,256]{2,1,0:T(8,128)(2,1)S(1)} all-to-all(bf16[8,128,256]{2,1,0:T(8,128)(2,1)S(1)} %get-tuple-element.30), channel_id=1, replica_groups={{0,8,16,24,32,40,48,56},{64,72,80,88,96,104,112,120},{128,136,144,152,1..., dimensions={0} | all-to-all | bytes 1048576 | tf_op jit(solution)/shard_map/all_to_all | solution.py:318
  57.4 0.3 shard_map.100
  57.7 7.3 %collective-permute-start.4 = (bf16[128,256]{1,0:T(8,128)(2,1)S(1)}, bf16[128,256]{1,0:T(8,128)(2,1)S(1)}, u32[]{:S(2)}, u32[]{:S(2)}) collective-permute-start(bf16[128,256]{1,0:T(8,128)(2,1)S(1)} %get-tuple-element.32), channel_id=1, source_target_pairs={{0,64},{64,128},{128,192},{192,256},{256,320},{320,384},{384,448},... | collective-permute-start | bytes 196616 | tf_op jit(solution)/shard_map/ppermute | solution.py:322
  65.0 1.9 %collective-permute-done.4.got_ref = bf16[128,256]{1,0:T(8,128)(2,1)S(1)} collective-permute-done((bf16[128,256]{1,0:T(8,128)(2,1)S(1)}, bf16[128,256]{1,0:T(8,128)(2,1)S(1)}, u32[]{:S(2)}, u32[]{:S(2)}) %collective-permute-start.4) | collective-permute-done | bytes 65568 | tf_op jit(solution)/shard_map/ppermute | solution.py:322
  66.9 0.7 shard_map.101
  (2 shorter events, 0.1 us)
Async XLA Ops:
  2.2 13.8 %all-to-all-start.1 = ((bf16[8,32,256]{2,1,0:T(8,128)(2,1)}), bf16[8,32,256]{2,1,0:T(8,128)(2,1)S(1)}, u32[]{:S(2)}, u32[]{:S(2)}) async-start(bf16[8,32,256]{2,1,0:T(8,128)(2,1)} %shard_map.95), calls=%async_computation.1 | async-start | bytes 262144 | tf_op jit(solution)/shard_map/all_to_all | solution.py:276
  16.0 20.3 %copy-start = (s32[8,128]{1,0:T(8,128)S(1)}, s32[8,128]{1,0:T(8,128)}, u32[]{:S(2)}) copy-start(s32[8,128]{1,0:T(8,128)} %get-tuple-element.24.start_ref) | copy-start | bytes 12292
  16.0 20.3 %all-to-all-start = ((bf16[8,32,2176]{2,1,0:T(8,128)(2,1)}), bf16[8,32,2176]{2,1,0:T(8,128)(2,1)S(1)}, u32[]{:S(2)}, u32[]{:S(2)}) async-start(bf16[8,32,2176]{2,1,0:T(8,128)(2,1)} %get-tuple-element.19), calls=%async_computation | async-start | bytes 2228224 | tf_op jit(solution)/shard_map/all_to_all | solution.py:276
  21.1 7.4 %collective-permute-start = (bf16[2,128,256]{2,1,0:T(8,128)(2,1)S(1)}, bf16[2,128,256]{2,1,0:T(8,128)(2,1)S(1)}, u32[]{:S(2)}, u32[]{:S(2)}) collective-permute-start(bf16[2,128,256]{2,1,0:T(8,128)(2,1)S(1)} %get-tuple-element.20.own_ref), channel_id=1, source_target_pairs={{0,8},{8,0},{16,24},{24,16},{32,40},{40,32},{48,56},{56,48},{64,72... | collective-permute-start | bytes 393224 | tf_op jit(solution)/shard_map/ppermute | solution.py:299
  28.6 9.7 %collective-permute-start.1 = (bf16[2,128,256]{2,1,0:T(8,128)(2,1)S(1)}, bf16[2,128,256]{2,1,0:T(8,128)(2,1)S(1)}, u32[]{:S(2)}, u32[]{:S(2)}) collective-permute-start(bf16[2,128,256]{2,1,0:T(8,128)(2,1)S(1)} %get-tuple-element.21), channel_id=1, source_target_pairs={{0,16},{8,24},{16,0},{24,8},{32,48},{40,56},{48,32},{56,40},{64,80... | collective-permute-start | bytes 393224 | tf_op jit(solution)/shard_map/ppermute | solution.py:302
  30.5 7.7 %collective-permute-start.2 = (bf16[2,128,256]{2,1,0:T(8,128)(2,1)S(1)}, bf16[2,128,256]{2,1,0:T(8,128)(2,1)S(1)}, u32[]{:S(2)}, u32[]{:S(2)}) collective-permute-start(bf16[2,128,256]{2,1,0:T(8,128)(2,1)S(1)} %get-tuple-element.22), channel_id=1, source_target_pairs={{16,32},{24,40},{32,16},{40,24},{48,64},{56,72},{64,48},{72,56},{8... | collective-permute-start | bytes 393224 | tf_op jit(solution)/shard_map/ppermute | solution.py:303
  31.2 7.0 %collective-permute-start.3 = (bf16[128,256]{1,0:T(8,128)(2,1)S(1)}, bf16[128,256]{1,0:T(8,128)(2,1)S(1)}, u32[]{:S(2)}, u32[]{:S(2)}) collective-permute-start(bf16[128,256]{1,0:T(8,128)(2,1)S(1)} %get-tuple-element.23), channel_id=1, source_target_pairs={{8,32},{24,48},{40,64},{56,80},{72,96},{88,112},{104,128},{120,144... | collective-permute-start | bytes 196616 | tf_op jit(solution)/shard_map/ppermute | solution.py:300
  57.7 9.2 %collective-permute-start.4 = (bf16[128,256]{1,0:T(8,128)(2,1)S(1)}, bf16[128,256]{1,0:T(8,128)(2,1)S(1)}, u32[]{:S(2)}, u32[]{:S(2)}) collective-permute-start(bf16[128,256]{1,0:T(8,128)(2,1)S(1)} %get-tuple-element.32), channel_id=1, source_target_pairs={{0,64},{64,128},{128,192},{192,256},{256,320},{320,384},{384,448},... | collective-permute-start | bytes 196616 | tf_op jit(solution)/shard_map/ppermute | solution.py:322

commit v4 on v3

--- a/solution.py
+++ b/solution.py
@@ -122,7 +122,7 @@
     return pl.ds(pl.multiple_of(half * 16, 16), 16)
 
 
-def tile_gradients(rows_ref, stat_ref, start_ref, half, backs, tiles, put_query):
+def tile_gradients(rows_ref, stat_ref, start_ref, half, backs, tiles, put_scores):
     key_at = lax.broadcasted_iota(jnp.int32, (BLOCK, BLOCK), 0)
     row_at = lax.broadcasted_iota(jnp.int32, (BLOCK, BLOCK), 1)
     start = start_ref[pl.ds(half, 1), :]
@@ -154,7 +154,7 @@
         score_grad = (weights * (weight_grad - delta)).astype(BF)
         value_total += dot(weights.astype(BF), grad, (1, 0))
         key_total += dot(score_grad, query, (1, 0))
-        put_query(g, dot(keys_turned, score_grad, (1, 0)))
+        put_scores(g, score_grad, keys_turned)
     return key_total * INV_ROOT, value_total
 
 
@@ -172,12 +172,13 @@
         stat_ref[half, 0] = (stat_turned[0:8, :] + stat_turned[8:16, :]) * LOG2E
         stat_ref[half, 1] = stat_turned[16:24, :] + stat_turned[24:32, :]
 
-        def put(g, part):
-            turned[half, :, g * HEAD : (g + 2) * HEAD] = part
-
         tiles, backs = [own_ref[half]], (0,)
         if mated:
             tiles, backs = tiles + [mate_ref[half]], (0, 1)
+
+        def put(g, scores, keys_turned):
+            turned[half, :, g * HEAD : (g + 2) * HEAD] = dot(keys_turned, scores, (1, 0))
+
         key_total, value_total = tile_gradients(
             rows_ref, stat_ref, start_ref, half, backs, tiles, put
         )
@@ -188,26 +189,24 @@
             near_out[:, HEAD:] = value_total[BLOCK:].astype(BF)
 
 
+def far_tiles(first_ref, second_ref, third_ref, mated, half):
+    swapped = lax.rem(lax.div(lax.axis_index("ctx"), 2), 2) == 1
+    from_first = swapped == (half == 0)
+    tiles = [jnp.where(from_first, first_ref[s], second_ref[s]) for s in range(2)]
+    return (tiles, (2, 3)) if mated else (tiles + [third_ref[...]], (1, 2, 3))
+
+
 def far_gradients(
-    rows_ref, first_ref, second_ref, third_ref, stat_ref, start_ref, turned, near_ref,
-    query_out, send_ref,
+    rows_ref, first_ref, second_ref, third_ref, stat_ref, start_ref, near_ref,
+    score_out, send_ref,
 ):
-    ctx = lax.axis_index("ctx")
-    member = lax.rem(ctx, 8)
-    swapped = lax.rem(lax.div(ctx, 2), 2) == 1
+    member = lax.rem(lax.axis_index("ctx"), 8)
     for mated, half in zip((True, False), halves()):
-        from_first = swapped == (half == 0)
-        tiles = [jnp.where(from_first, first_ref[s], second_ref[s]) for s in range(2)]
-        backs = (2, 3)
-        if not mated:
-            tiles, backs = tiles + [third_ref[...]], (1, 2, 3)
-
-        def put(g, part):
-            part = (part + turned[half, :, g * HEAD : (g + 2) * HEAD]) * INV_ROOT
-            for n in range(2):
-                query_out[half, :, (g + n) * HEAD : (g + n + 1) * HEAD] = (
-                    part[:, n * HEAD : (n + 1) * HEAD].T.astype(BF)
-                )
+        tiles, backs = far_tiles(first_ref, second_ref, third_ref, mated, half)
+        keys_at = slice(0, 2 * BLOCK) if mated else slice(2 * BLOCK, 5 * BLOCK)
+
+        def put(g, scores, keys_turned):
+            score_out[keys_at, g * HEAD : (g + 2) * HEAD] = scores
 
         key_total, value_total = tile_gradients(
             rows_ref, stat_ref, start_ref, half, backs, tiles, put
@@ -224,6 +223,21 @@
             send_ref[slot(back), :, HEAD:] = value_total[part].astype(BF)
     for apart in (0, 4):
         send_ref[lax.rem(member + apart, 8)] = jnp.zeros((BLOCK, 2 * HEAD), BF)
+
+
+def query_gradients(first_ref, second_ref, third_ref, score_ref, turned, query_out):
+    for mated, half in zip((True, False), halves()):
+        tiles, _ = far_tiles(first_ref, second_ref, third_ref, mated, half)
+        keys_at = slice(0, 2 * BLOCK) if mated else slice(2 * BLOCK, 5 * BLOCK)
+        keys_turned = jnp.concatenate([t[:, :HEAD] for t in tiles], axis=0).T
+        for g in range(0, GROUP, 2):
+            columns = slice(g * HEAD, (g + 2) * HEAD)
+            part = dot(keys_turned, score_ref[keys_at, columns], (1, 0))
+            part = (part + turned[half, :, columns]) * INV_ROOT
+            for n in range(2):
+                query_out[half, :, (g + n) * HEAD : (g + n + 1) * HEAD] = (
+                    part[:, n * HEAD : (n + 1) * HEAD].T.astype(BF)
+                )
 
 
 def add_group(own_ref, got_ref, sum_ref, pass_ref):
@@ -312,11 +326,14 @@
         4,
         scratch=[pltpu.VMEM((HEAD, BLOCK), F32)],
     )(large, held, mate, starts)
-    query_grad, sent = call(
-        far_gradients, [((2, BLOCK, 1024), BF), ((8, BLOCK, 256), BF)], 8
-    )(large, first, second, third, stats, starts, turned, near)
+    scores, sent = call(
+        far_gradients, [((5 * BLOCK, 1024), BF), ((8, BLOCK, 256), BF)], 7
+    )(large, first, second, third, stats, starts, near)
     got = lax.all_to_all(
         sent, "ctx", split_axis=0, concat_axis=0, tiled=True, axis_index_groups=groups
+    )
+    (query_grad,) = call(query_gradients, [((2, BLOCK, 1024), BF)], 5)(
+        first, second, third, scores, turned
     )
     sums, passed = call(add_group, [((2, BLOCK, 256), F32), tile], 2)(own, got)
     passed = lax.ppermute(passed, "ctx", between_groups())

time: 68.1 us -> 66.9 us (0.982)
  waiting for transfers between devices: 12.9 us -> 11.6 us
    ppermute x1, waiting for transfers between devices: 1.88 us -> 0.59 us  [body(): passed = lax.ppermute(passed, 'ctx', between_groups())]
    pallas_call x1 -> x2, Pallas kernels: 3.19 us -> 3.24 us  [the longest x1 1.95 us: body(): call(far_gradients, [((5 * BLOCK, 1024), BF), ((8, BLOCK, 256), BF)], 7)]
  transfers between devices with their start and end apart: 7 -> 7, of which waited for: 4 -> 4; matrix products, arithmetic and copies ran while one was open for 0% -> 0% of each run, Pallas kernels for 8% -> 10%
where the time goes in v4:
time: 66.9 us; the launch traced here: 66.4 us
  starting transfers between devices  26.7 us (40%)
  blocking collectives  16 us (24%)
  waiting for transfers between devices  11.6 us (17%)
  Pallas kernels  11.4 us (17%)
  between operations  0.74 us (1%)
    all_to_all x1, blocking collectives, body(): lax.all_to_all(sent, 'ctx', split_axis=0, concat_axis=0, tiled=True, axis...  16 us
    all_to_all x2, starting transfers between devices, by_head(): return lax.all_to_all(x, 'kvh', split_axis=0, concat_axis=0, tiled=True)  14.2 us
    ppermute x1, starting transfers between devices, body(): passed = lax.ppermute(passed, 'ctx', between_groups())  7.33 us
    ppermute x1, waiting for transfers between devices, body(): mate = lax.ppermute(held, 'ctx', mates)  5.52 us
    all_to_all x2, waiting for transfers between devices, by_head(): return lax.all_to_all(x, 'kvh', split_axis=0, concat_axis=0, tiled=True)  5.48 us
    pallas_call x1, Pallas kernels, body(): call(pack_large, [((8, 32, 2176), BF), ((8, BLOCK), jnp.int32)], 5, smem=...  3.67 us
    pallas_call x1, Pallas kernels, body(): call(far_gradients, [((5 * BLOCK, 1024), BF), ((8, BLOCK, 256), BF)], 7)  1.95 us
    ppermute x1, starting transfers between devices, body(): mate = lax.ppermute(held, 'ctx', mates)  1.92 us
  transfers between devices with their start and end apart: 7, of which 4 were waited for; matrix products, arithmetic and copies ran while one was open for 0% of the time, Pallas kernels for 10%

profile of v4, /device:TPU:8, one launch (start us, length us, event | category | flops | bytes accessed | tf_op | source)
XLA Modules:
  0.0 66.4 jit_solution(3255601713504506512)
XLA Ops:
  0.6 1.6 %shard_map.94 = bf16[8,32,256]{2,1,0:T(8,128)(2,1)} custom-call(bf16[2,16,1024]{2,1,0:T(8,128)(2,1)} %key_raw.1, bf16[2,16,1024]{2,1,0:T(8,128)(2,1)} %value_raw.1), custom_call_target="tpu_custom_call" | custom-call | tf_op jit(solution)/shard_map/pallas_call | solution.py:292
  2.2 9.1 %all-to-all-start = ((bf16[8,32,256]{2,1,0:T(8,128)(2,1)}), bf16[8,32,256]{2,1,0:T(8,128)(2,1)S(1)}, u32[]{:S(2)}, u32[]{:S(2)}) async-start(bf16[8,32,256]{2,1,0:T(8,128)(2,1)} %shard_map.94), calls=%async_computation | async-start | bytes 262144 | tf_op jit(solution)/shard_map/all_to_all | solution.py:290
  11.3 3.7 %shard_map.97 = (bf16[8,32,2176]{2,1,0:T(8,128)(2,1)}, s32[8,128]{1,0:T(8,128)}) custom-call(s32[64]{0:T(128)} %length_ref.1, bf16[2,16,8192]{2,1,0:T(8,128)(2,1)} %refs_0_.1, bf16[2,16,8192]{2,1,0:T(8,128)(2,1)} %refs_1_.1, bf16[2,16,8192]{2,1,0:T(8,128)(2,1)} %refs_2_.1, f32[2,16,64]{2,1,0:T(8,128)} %refs_3_.1), custom_call_target="tpu_custom_call" | custom-call | tf_op jit(solution)/shard_map/pallas_call | solution.py:300
  15.0 1.0 %all-to-all-done.packed_ref = bf16[8,32,256]{2,1,0:T(8,128)(2,1)S(1)} async-done(((bf16[8,32,256]{2,1,0:T(8,128)(2,1)}), bf16[8,32,256]{2,1,0:T(8,128)(2,1)S(1)}, u32[]{:S(2)}, u32[]{:S(2)}) %all-to-all-start) | async-done | bytes 131104 | tf_op jit(solution)/shard_map/all_to_all | solution.py:290
  16.0 0.0 copy-start
  16.0 5.0 %all-to-all-start.1 = ((bf16[8,32,2176]{2,1,0:T(8,128)(2,1)}), bf16[8,32,2176]{2,1,0:T(8,128)(2,1)S(1)}, u32[]{:S(2)}, u32[]{:S(2)}) async-start(bf16[8,32,2176]{2,1,0:T(8,128)(2,1)} %get-tuple-element.23), calls=%async_computation.1 | async-start | bytes 2228224 | tf_op jit(solution)/shard_map/all_to_all | solution.py:290
  21.1 1.9 %collective-permute-start = (bf16[2,128,256]{2,1,0:T(8,128)(2,1)S(1)}, bf16[2,128,256]{2,1,0:T(8,128)(2,1)S(1)}, u32[]{:S(2)}, u32[]{:S(2)}) collective-permute-start(bf16[2,128,256]{2,1,0:T(8,128)(2,1)S(1)} %get-tuple-element.19.own_ref), channel_id=1, source_target_pairs={{0,8},{8,0},{16,24},{24,16},{32,40},{40,32},{48,56},{56,48},{64,72... | collective-permute-start | bytes 393224 | tf_op jit(solution)/shard_map/ppermute | solution.py:313
  23.0 5.5 %collective-permute-done.mate_ref = bf16[2,128,256]{2,1,0:T(8,128)(2,1)S(1)} collective-permute-done((bf16[2,128,256]{2,1,0:T(8,128)(2,1)S(1)}, bf16[2,128,256]{2,1,0:T(8,128)(2,1)S(1)}, u32[]{:S(2)}, u32[]{:S(2)}) %collective-permute-start) | collective-permute-done | bytes 131104 | tf_op jit(solution)/shard_map/ppermute | solution.py:313
  28.6 1.9 %collective-permute-start.1 = (bf16[2,128,256]{2,1,0:T(8,128)(2,1)S(1)}, bf16[2,128,256]{2,1,0:T(8,128)(2,1)S(1)}, u32[]{:S(2)}, u32[]{:S(2)}) collective-permute-start(bf16[2,128,256]{2,1,0:T(8,128)(2,1)S(1)} %get-tuple-element.20), channel_id=1, source_target_pairs={{0,16},{8,24},{16,0},{24,8},{32,48},{40,56},{48,32},{56,40},{64,80... | collective-permute-start | bytes 393224 | tf_op jit(solution)/shard_map/ppermute | solution.py:316
  30.5 0.7 %collective-permute-start.2 = (bf16[2,128,256]{2,1,0:T(8,128)(2,1)S(1)}, bf16[2,128,256]{2,1,0:T(8,128)(2,1)S(1)}, u32[]{:S(2)}, u32[]{:S(2)}) collective-permute-start(bf16[2,128,256]{2,1,0:T(8,128)(2,1)S(1)} %get-tuple-element.21), channel_id=1, source_target_pairs={{16,32},{24,40},{32,16},{40,24},{48,64},{56,72},{64,48},{72,56},{8... | collective-permute-start | bytes 393224 | tf_op jit(solution)/shard_map/ppermute | solution.py:317
  31.2 0.7 %collective-permute-start.3 = (bf16[128,256]{1,0:T(8,128)(2,1)S(1)}, bf16[128,256]{1,0:T(8,128)(2,1)S(1)}, u32[]{:S(2)}, u32[]{:S(2)}) collective-permute-start(bf16[128,256]{1,0:T(8,128)(2,1)S(1)} %get-tuple-element.22), channel_id=1, source_target_pairs={{8,32},{24,48},{40,64},{56,80},{72,96},{88,112},{104,128},{120,144... | collective-permute-start | bytes 196616 | tf_op jit(solution)/shard_map/ppermute | solution.py:314
  31.9 4.4 %all-to-all-done.1.rows_ref = bf16[8,32,2176]{2,1,0:T(8,128)(2,1)S(1)} async-done(((bf16[8,32,2176]{2,1,0:T(8,128)(2,1)}), bf16[8,32,2176]{2,1,0:T(8,128)(2,1)S(1)}, u32[]{:S(2)}, u32[]{:S(2)}) %all-to-all-start.1) | async-done | bytes 1114144 | tf_op jit(solution)/shard_map/all_to_all | solution.py:290
  36.3 0.0 copy-done
  36.3 1.9 %shard_map.98 = (f32[2,128,1024]{2,1,0:T(8,128)S(1)}, f32[2,128,256]{2,1,0:T(8,128)S(1)}, bf16[128,256]{1,0:T(8,128)(2,1)S(1)}, f32[2,2,8,128]{3,2,1,0:T(8,128)S(1)}) custom-call(bf16[8,32,2176]{2,1,0:T(8,128)(2,1)S(1)} %all-to-all-done.1.rows_ref, bf16[2,128,256]{2,1,0:T(8,128)(2,1)S(1)} %get-tuple-element.19.own_ref, ...), custom_call_target="tpu_custom_call" | custom-call | tf_op jit(solution)/shard_map/pallas_call | solution.py:318
  38.2 0.0 collective-permute-done.3.third_ref
  38.2 0.0 collective-permute-done.1.first_ref
  38.3 0.0 collective-permute-done.2.second_ref
  38.3 1.9 %shard_map.99 = (bf16[640,1024]{1,0:T(8,128)(2,1)S(1)}, bf16[8,128,256]{2,1,0:T(8,128)(2,1)S(1)}) custom-call(bf16[8,32,2176]{2,1,0:T(8,128)(2,1)S(1)} %all-to-all-done.1.rows_ref, bf16[2,128,256]{2,1,0:T(8,128)(2,1)S(1)} %collective-permute-done.1.first_ref, bf16[2,128,256]{2,1,0:T(8,128)(2,1)S(1)} %collective-permute-done.2.second_ref, ...), custom_call_target="tpu_custom_call" | custom-call | tf_op jit(solution)/shard_map/pallas_call | solution.py:329
  40.2 16.0 %all_to_all.15.got_ref = bf16[8,128,256]{2,1,0:T(8,128)(2,1)S(1)} all-to-all(bf16[8,128,256]{2,1,0:T(8,128)(2,1)S(1)} %get-tuple-element.30), channel_id=1, replica_groups={{0,8,16,24,32,40,48,56},{64,72,80,88,96,104,112,120},{128,136,144,152,1..., dimensions={0} | all-to-all | bytes 1048576 | tf_op jit(solution)/shard_map/all_to_all | solution.py:332
  56.2 0.3 shard_map.101
  56.5 7.3 %collective-permute-start.4 = (bf16[128,256]{1,0:T(8,128)(2,1)S(1)}, bf16[128,256]{1,0:T(8,128)(2,1)S(1)}, u32[]{:S(2)}, u32[]{:S(2)}) collective-permute-start(bf16[128,256]{1,0:T(8,128)(2,1)S(1)} %get-tuple-element.32), channel_id=1, source_target_pairs={{0,64},{64,128},{128,192},{192,256},{256,320},{320,384},{384,448},... | collective-permute-start | bytes 196616 | tf_op jit(solution)/shard_map/ppermute | solution.py:339
  63.8 1.3 %shard_map.100 = bf16[2,128,1024]{2,1,0:T(8,128)(2,1)} custom-call(bf16[2,128,256]{2,1,0:T(8,128)(2,1)S(1)} %collective-permute-done.1.first_ref, bf16[2,128,256]{2,1,0:T(8,128)(2,1)S(1)} %collective-permute-done.2.second_ref, bf16[128,256]{1,0:T(8,128)(2,1)S(1)} %collective-permute-done.3.third_ref, bf16[640,1024]{1,0:T(8,128)(2,1)S(1)} %get-tuple-element.27.score_ref, ...), custom_call_target="tpu_custom_call" | custom-call | tf_op jit(solution)/shard_map/pallas_call | solution.py:335
  65.1 0.6 collective-permute-done.4.got_ref
  65.7 0.7 %shard_map.102 = (bf16[2,128,128]{2,1,0:T(8,128)(2,1)}, bf16[2,128,128]{2,1,0:T(8,128)(2,1)}) custom-call(f32[2,128,256]{2,1,0:T(8,128)S(1)} %get-tuple-element.31.sum_ref, bf16[128,256]{1,0:T(8,128)(2,1)S(1)} %collective-permute-done.4.got_ref), custom_call_target="tpu_custom_call" | custom-call | tf_op jit(solution)/shard_map/pallas_call | solution.py:340
  (2 shorter events, 0.1 us)
Async XLA Ops:
  2.2 13.8 %all-to-all-start = ((bf16[8,32,256]{2,1,0:T(8,128)(2,1)}), bf16[8,32,256]{2,1,0:T(8,128)(2,1)S(1)}, u32[]{:S(2)}, u32[]{:S(2)}) async-start(bf16[8,32,256]{2,1,0:T(8,128)(2,1)} %shard_map.94), calls=%async_computation | async-start | bytes 262144 | tf_op jit(solution)/shard_map/all_to_all | solution.py:290
  16.0 20.3 %copy-start = (s32[8,128]{1,0:T(8,128)S(1)}, s32[8,128]{1,0:T(8,128)}, u32[]{:S(2)}) copy-start(s32[8,128]{1,0:T(8,128)} %get-tuple-element.24.start_ref) | copy-start | bytes 12292
  16.0 20.3 %all-to-all-start.1 = ((bf16[8,32,2176]{2,1,0:T(8,128)(2,1)}), bf16[8,32,2176]{2,1,0:T(8,128)(2,1)S(1)}, u32[]{:S(2)}, u32[]{:S(2)}) async-start(bf16[8,32,2176]{2,1,0:T(8,128)(2,1)} %get-tuple-element.23), calls=%async_computation.1 | async-start | bytes 2228224 | tf_op jit(solution)/shard_map/all_to_all | solution.py:290
  21.1 7.4 %collective-permute-start = (bf16[2,128,256]{2,1,0:T(8,128)(2,1)S(1)}, bf16[2,128,256]{2,1,0:T(8,128)(2,1)S(1)}, u32[]{:S(2)}, u32[]{:S(2)}) collective-permute-start(bf16[2,128,256]{2,1,0:T(8,128)(2,1)S(1)} %get-tuple-element.19.own_ref), channel_id=1, source_target_pairs={{0,8},{8,0},{16,24},{24,16},{32,40},{40,32},{48,56},{56,48},{64,72... | collective-permute-start | bytes 393224 | tf_op jit(solution)/shard_map/ppermute | solution.py:313
  28.6 9.7 %collective-permute-start.1 = (bf16[2,128,256]{2,1,0:T(8,128)(2,1)S(1)}, bf16[2,128,256]{2,1,0:T(8,128)(2,1)S(1)}, u32[]{:S(2)}, u32[]{:S(2)}) collective-permute-start(bf16[2,128,256]{2,1,0:T(8,128)(2,1)S(1)} %get-tuple-element.20), channel_id=1, source_target_pairs={{0,16},{8,24},{16,0},{24,8},{32,48},{40,56},{48,32},{56,40},{64,80... | collective-permute-start | bytes 393224 | tf_op jit(solution)/shard_map/ppermute | solution.py:316
  30.5 7.7 %collective-permute-start.2 = (bf16[2,128,256]{2,1,0:T(8,128)(2,1)S(1)}, bf16[2,128,256]{2,1,0:T(8,128)(2,1)S(1)}, u32[]{:S(2)}, u32[]{:S(2)}) collective-permute-start(bf16[2,128,256]{2,1,0:T(8,128)(2,1)S(1)} %get-tuple-element.21), channel_id=1, source_target_pairs={{16,32},{24,40},{32,16},{40,24},{48,64},{56,72},{64,48},{72,56},{8... | collective-permute-start | bytes 393224 | tf_op jit(solution)/shard_map/ppermute | solution.py:317
  31.2 7.0 %collective-permute-start.3 = (bf16[128,256]{1,0:T(8,128)(2,1)S(1)}, bf16[128,256]{1,0:T(8,128)(2,1)S(1)}, u32[]{:S(2)}, u32[]{:S(2)}) collective-permute-start(bf16[128,256]{1,0:T(8,128)(2,1)S(1)} %get-tuple-element.22), channel_id=1, source_target_pairs={{8,32},{24,48},{40,64},{56,80},{72,96},{88,112},{104,128},{120,144... | collective-permute-start | bytes 196616 | tf_op jit(solution)/shard_map/ppermute | solution.py:314
  56.5 9.2 %collective-permute-start.4 = (bf16[128,256]{1,0:T(8,128)(2,1)S(1)}, bf16[128,256]{1,0:T(8,128)(2,1)S(1)}, u32[]{:S(2)}, u32[]{:S(2)}) collective-permute-start(bf16[128,256]{1,0:T(8,128)(2,1)S(1)} %get-tuple-element.32), channel_id=1, source_target_pairs={{0,64},{64,128},{128,192},{192,256},{256,320},{320,384},{384,448},... | collective-permute-start | bytes 196616 | tf_op jit(solution)/shard_map/ppermute | solution.py:339
